TPU v7x, 512 devices: a whole 4x8x8 slice. The times are simulated.
512 devices in a mesh: band: 32 (over x, y), gate: 16 (over z, core).
Axes of the slice: x: 4, y: 8, z: 8, core: 2. Of those that a mesh axis runs over, the one named last changes fastest.
Arguments:
- messages: bfloat16 [4, 32, 2, 2048, 256], P(None, 'band', None, 'gate'), may hold values from -6 to 6
- gate_type: int32 [4, 32, 2, 2048], P(None, 'band', None, 'gate'), may hold values from 0 to 7
- state_grad: bfloat16 [4, 32, 2, 2048, 256], P(None, 'band', None, 'gate'), may hold values from -6 to 6
- fanin_owner: int32 [4, 32, 2, 2048, 4], P(None, 'band', None, 'gate'), may hold values from 0 to 15, all different within a row; in each aligned block of 128 rows (0 to 127, 128 to 255, ..., all dimensions but the last counted through in order) at most 48 rows name the same one
- fanin_slot: int32 [4, 32, 2, 2048, 4], P(None, 'band', None, 'gate'), may hold values from 0 to 127
- live_count: int32 [4, 32, 2], P(None, 'band'), may hold values from 1024 to 2048, as said below
- hidden_weight: bfloat16 [256, 768], replicated, may hold values from -0.375 to 0.375
- hidden_bias: float32 [768], replicated, may hold values from -3 to 3
- type_table: float32 [8, 768], replicated, may hold values from -6 to 6
Outputs:
- input_grad: bfloat16 [4, 32, 2048, 256], P(None, 'band', 'gate')
- weight_grad: float32 [256, 768], replicated
- bias_grad: float32 [768], replicated
- table_grad: float32 [8, 768], replicated
Inputs may be any that keep to these rules, and one draw needn't show every extreme that they name: `fanin_owner`: the 4 fanins of a gate lie on 4 different devices of the gate axis; among the gates of one device (aligned blocks of 128 gates of a level), at most 48 fanins lie on any one device, and exactly 48 on some. `live_count`: gates of a level whose index is below the count are live, the others are padding.
All inputs are finite; a program needn't handle non-finite values.
Results may differ from a plain program's by a relative error of at most 0.0069.
Values may be sent and summed in bfloat16 or wider, within the bound.
A program may use at most 128 MiB of HBM per device.

v0:
```python
import math

import jax
import jax.numpy as jnp
from jax import lax
from jax.sharding import PartitionSpec as P


def passed_along(value, axis, steps):
    count = lax.axis_size(axis)
    first, last = (max(0, -steps), min(count, count - steps))
    return lax.ppermute(value, axis, [(source, source + steps) for source in range(first, last)])


def cell_forward(message, kinds, type_rows, weight, bias_row):
    width = message.shape[-1]
    one_hot = (kinds[:, None] == jnp.arange(type_rows.shape[0], dtype=jnp.int32)[None, :]).astype(
        jnp.float32
    )
    pre_acts = jnp.dot(message, weight, preferred_element_type=jnp.float32) + bias_row
    inputs = jnp.dot(one_hot, type_rows, precision=lax.Precision.HIGHEST)
    reset_gate = jax.nn.sigmoid(inputs[:, :width] + pre_acts[:, :width])
    update_gate = jax.nn.sigmoid(inputs[:, width : 2 * width] + pre_acts[:, width : 2 * width])
    candidate = pre_acts[:, 2 * width :]
    new_state = jnp.tanh(inputs[:, 2 * width :] + reset_gate * candidate)
    return (message.astype(jnp.float32), reset_gate, update_gate, candidate, new_state, one_hot)


def cell_backward(cache, state_cot, live, weight):
    message_f, reset_gate, update_gate, candidate, new_state, one_hot = cache
    state_cot = jnp.where(live[:, None], state_cot, 0.0)
    new_pre = state_cot * (1.0 - update_gate) * (1.0 - new_state * new_state)
    reset_pre = new_pre * candidate * reset_gate * (1.0 - reset_gate)
    update_pre = state_cot * (message_f - new_state) * update_gate * (1.0 - update_gate)
    cand_grad = new_pre * reset_gate
    grad_acts = jnp.concatenate([reset_pre, update_pre, cand_grad], axis=1).astype(jnp.bfloat16)
    grad_inputs = jnp.concatenate(
        [grad_acts[:, : 2 * reset_pre.shape[1]], new_pre.astype(jnp.bfloat16)], axis=1
    )
    down_rows = state_cot * update_gate + lax.dot_general(
        grad_acts, weight, (((1,), (1,)), ((), ())), preferred_element_type=jnp.float32
    )
    return (grad_acts, grad_inputs, down_rows.astype(jnp.bfloat16))


def shards(
    messages,
    gate_type,
    state_grad,
    fanin_owner,
    fanin_slot,
    live_count,
    hidden_weight,
    hidden_bias,
    type_table,
):
    circuits, _, levels, per_device, fanins = fanin_owner.shape
    hidden = messages.shape[-1]
    groups = lax.axis_size("gate")
    my_index = lax.axis_index("gate")
    gate_ids = my_index * per_device + jnp.arange(per_device, dtype=jnp.int32)
    cached = [
        [
            cell_forward(
                messages[circuit, 0, level],
                gate_type[circuit, 0, level],
                type_table,
                hidden_weight,
                hidden_bias,
            )
            for level in range(levels)
        ]
        for circuit in range(circuits)
    ]
    slot_cap = min(per_device, 3 * per_device * fanins // (2 * groups))
    owners = fanin_owner[:, 0].reshape(circuits, levels, per_device * fanins)
    chosen = (owners[..., None] == jnp.arange(groups, dtype=jnp.int32)).astype(jnp.int32)
    slot_rank = jnp.sum((jnp.cumsum(chosen, axis=2) - chosen) * chosen, axis=3)
    offsets = owners * slot_cap + slot_rank
    table_base = (jnp.arange(circuits * levels, dtype=jnp.int32) * (groups * slot_cap)).reshape(
        circuits, levels, 1
    )
    tables = jnp.full((circuits * levels * groups * slot_cap,), per_device, jnp.int32)
    tables = tables.at[(offsets + table_base).reshape(-1)].set(fanin_slot[:, 0].reshape(-1))
    arrived = lax.all_to_all(
        tables.reshape(circuits, levels, groups, slot_cap),
        "gate",
        split_axis=2,
        concat_axis=2,
        tiled=True,
    )

    def deliver(circuit, level, down_rows):
        sending = jnp.zeros((groups * slot_cap, hidden), jnp.bfloat16)
        sending = sending.at[offsets[circuit, level]].set(jnp.repeat(down_rows, fanins, axis=0))
        received = lax.all_to_all(
            sending.reshape(groups, slot_cap, hidden),
            "gate",
            split_axis=0,
            concat_axis=0,
            tiled=True,
        )
        fanin_grad = jnp.zeros((per_device + 1, hidden), jnp.float32)
        fanin_grad = fanin_grad.at[arrived[circuit, level].reshape(-1)].add(
            received.reshape(-1, hidden).astype(jnp.float32)
        )
        return fanin_grad[:per_device]

    def band_pass(circuit, incoming, keep):
        state_cot = state_grad[circuit, 0, levels - 1].astype(jnp.float32) + incoming
        weight_sum = jnp.zeros((hidden, 3 * hidden), jnp.float32)
        bias_sum = jnp.zeros((3 * hidden,), jnp.float32)
        table_sum = jnp.zeros(type_table.shape, jnp.float32)
        fanin_grad = jnp.zeros((per_device, hidden), jnp.float32)
        for level in range(levels - 1, -1, -1):
            live = gate_ids < live_count[circuit, 0, level]
            cache = cached[circuit][level]
            grad_acts, grad_inputs, down_rows = cell_backward(cache, state_cot, live, hidden_weight)
            fanin_grad = deliver(circuit, level, down_rows)
            if keep:
                weight_sum = weight_sum + lax.dot_general(
                    messages[circuit, 0, level],
                    grad_acts,
                    (((0,), (0,)), ((), ())),
                    preferred_element_type=jnp.float32,
                )
                bias_sum = bias_sum + jnp.sum(grad_acts.astype(jnp.float32), axis=0)
                table_sum = table_sum + lax.dot_general(
                    cache[5],
                    grad_inputs.astype(jnp.float32),
                    (((0,), (0,)), ((), ())),
                    precision=lax.Precision.HIGHEST,
                )
            if level > 0:
                state_cot = state_grad[circuit, 0, level - 1].astype(jnp.float32) + fanin_grad
        return (fanin_grad.astype(jnp.bfloat16), weight_sum, bias_sum, table_sum)

    silent = jnp.zeros((per_device, hidden), jnp.float32)
    arriving = []
    firsts = jnp.stack([band_pass(circuit, silent, False)[0] for circuit in range(circuits)])
    moved = passed_along(firsts, "band", -1)
    arriving = [moved[circuit] for circuit in range(circuits)]
    finals = []
    weight_total = jnp.zeros((hidden, 3 * hidden), jnp.float32)
    bias_total = jnp.zeros((3 * hidden,), jnp.float32)
    table_total = jnp.zeros(type_table.shape, jnp.float32)
    for circuit in range(circuits):
        final, weight_sum, bias_sum, table_sum = band_pass(
            circuit, arriving[circuit].astype(jnp.float32), True
        )
        finals.append(final)
        weight_total = weight_total + weight_sum
        bias_total = bias_total + bias_sum
        table_total = table_total + table_sum
    weight_total, bias_total, table_total = lax.psum(
        (weight_total, bias_total, table_total), ("band", "gate")
    )
    scale = 1.0 / math.sqrt(circuits * lax.axis_size("band") * levels * per_device * groups)
    return (
        jnp.stack(finals)[:, None],
        weight_total * scale,
        bias_total * scale,
        table_total * scale,
    )


def solution(mesh):
    return jax.shard_map(
        shards,
        mesh=mesh,
        in_specs=(
            P(None, "band", None, "gate", None),
            P(None, "band", None, "gate"),
            P(None, "band", None, "gate", None),
            P(None, "band", None, "gate", None),
            P(None, "band", None, "gate", None),
            P(None, "band", None),
            P(),
            P(),
            P(),
        ),
        out_specs=(P(None, "band", "gate", None), P(), P(), P()),
        check_vma=False,
    )
```

profile of v0, /device:TPU:1, one launch (start us, length us, event | category | flops | bytes accessed | tf_op | source)
XLA Modules:
  0.0 725.2 jit_solution(9332243323328404468)
XLA Ops:
  9.2 9.1 %reduce-window.6 = s32[4,2,16,4,128]{4,2,3,1,0:T(8,128)S(1)} reduce-window(s32[4,2,16,4,128]{4,2,3,1,0:T(8,128)S(1)} %fusion.58, s32[]{:T(128)} %constant.15.clone.1), window={size=1x1x1x1x128 pad=0_0x0_0x0_0x0_0x127_0}, to_apply=%region_0.0 | reduce-window | flops 8323072 | bytes 524292 | tf_op jit(solution)/shard_map/reduce-window
  21.2 15.5 %scatter_custom_fusion = s32[6144]{0:T(1024)S(1)} fusion(s32[4096]{0:T(1024)S(1)} %bitcast.436, s32[4096]{0:T(1024)S(1)} %reshape.794, s32[]{:T(128)} %constant.13.clone.1), kind=kCustom, calls=%fused_computation.587 | custom fusion | bytes 24580 | tf_op jit(solution)/shard_map/scatter | solution.py:84
  37.7 11.8 %all-to-all-start = ((s32[16,1,384]{2,1,0:T(1,128)}), s32[16,1,384]{2,1,0:T(1,128)S(1)}, u32[]{:S(2)}, u32[]{:S(2)}) async-start(s32[16,1,384]{2,1,0:T(1,128)} %reshape.1171), calls=%async_computation | async-start | bytes 49152 | tf_op jit(solution)/shard_map/all_to_all | solution.py:85
  62.6 3.4 scatter_custom_fusion.13
  66.6 7.2 all-to-all-start.7
  75.8 3.6 scatter_custom_fusion.1
  82.0 6.6 all-to-all-done.7
  88.5 4.1 all-to-all-start.1
  99.0 7.5 %scatter_custom_fusion.14 = f32[129,256]{1,0:T(8,128)} fusion(s32[768]{0:T(1024)S(1)} %fusion.356, bf16[768,256]{1,0:T(8,128)(2,1)} %bitcast.111, f32[]{:T(128)} %constant.12.clone.1), kind=kCustom, calls=%fused_computation.106 | custom fusion | flops 393216 | bytes 525316 | tf_op jit(solution)/shard_map/scatter-add | solution.py:104
  106.4 7.5 %scatter_custom_fusion.2 = f32[129,256]{1,0:T(8,128)} fusion(s32[768]{0:T(1024)S(1)} %fusion.350, bf16[768,256]{1,0:T(8,128)(2,1)} %bitcast.105, f32[]{:T(128)} %constant.12.clone.1), kind=kCustom, calls=%fused_computation.118 | custom fusion | flops 393216 | bytes 525316 | tf_op jit(solution)/shard_map/scatter-add | solution.py:104
  114.0 2.5 multiply_convert_fusion.41
  119.2 3.4 scatter_custom_fusion.9
  122.6 6.8 all-to-all-start.5
  135.1 3.5 scatter_custom_fusion.5
  138.6 5.4 all-to-all-done.5
  143.9 3.5 all-to-all-start.3
  157.4 3.5 scatter_custom_fusion.3
  160.9 7.5 %scatter_custom_fusion.10 = f32[129,256]{1,0:T(8,128)} fusion(s32[768]{0:T(1024)} %fusion.354, bf16[768,256]{1,0:T(8,128)(2,1)} %bitcast.109, f32[]{:T(128)} %constant.12.clone.1), kind=kCustom, calls=%fused_computation.110 | custom fusion | flops 393216 | bytes 525824 | tf_op jit(solution)/shard_map/scatter-add | solution.py:104
  169.1 6.5 all-to-all-start.2
  175.6 7.7 %scatter_custom_fusion.6 = f32[129,256]{1,0:T(8,128)} fusion(s32[768]{0:T(1024)} %fusion.352, bf16[768,256]{1,0:T(8,128)(2,1)} %bitcast.425, f32[]{:T(128)} %constant.12.clone.1), kind=kCustom, calls=%fused_computation.114 | custom fusion | flops 393216 | bytes 525824 | tf_op jit(solution)/shard_map/scatter-add | solution.py:104
  184.0 2.2 multiply_convert_fusion.36
  191.5 3.5 scatter_custom_fusion.7
  194.9 7.1 all-to-all-start.4
  206.0 3.5 scatter_custom_fusion.11
  209.5 7.2 all-to-all-done.4
  216.7 4.1 all-to-all-start.6
  230.4 1.7 reshape.914
  232.1 3.5 scatter_custom_fusion.15
  235.5 6.3 all-to-all-start.8
  241.9 7.7 %scatter_custom_fusion.4 = f32[129,256]{1,0:T(8,128)} fusion(s32[768]{0:T(1024)} %fusion.349, bf16[768,256]{1,0:T(8,128)(2,1)} %bitcast.106, f32[]{:T(128)} %constant.12.clone.1), kind=kCustom, calls=%fused_computation.116 | custom fusion | flops 393216 | bytes 525824 | tf_op jit(solution)/shard_map/scatter-add | solution.py:104
  251.2 7.4 %scatter_custom_fusion.8 = f32[129,256]{1,0:T(8,128)} fusion(s32[768]{0:T(1024)} %fusion.351, bf16[768,256]{1,0:T(8,128)(2,1)} %bitcast.108, f32[]{:T(128)} %constant.12.clone.1), kind=kCustom, calls=%fused_computation.112 | custom fusion | flops 393216 | bytes 525824 | tf_op jit(solution)/shard_map/scatter-add | solution.py:104
  258.6 7.4 %scatter_custom_fusion.12 = f32[129,256]{1,0:T(8,128)} fusion(s32[768]{0:T(1024)} %fusion.353, bf16[768,256]{1,0:T(8,128)(2,1)} %bitcast.110, f32[]{:T(128)} %constant.12.clone.1), kind=kCustom, calls=%fused_computation.108 | custom fusion | flops 393216 | bytes 525824 | tf_op jit(solution)/shard_map/scatter-add | solution.py:104
  269.1 7.4 %scatter_custom_fusion.16 = f32[129,256]{1,0:T(8,128)} fusion(s32[768]{0:T(1024)S(1)} %fusion.355, bf16[768,256]{1,0:T(8,128)(2,1)} %bitcast.112, f32[]{:T(128)} %constant.12.clone.1), kind=kCustom, calls=%fused_computation.104 | custom fusion | flops 393216 | bytes 525316 | tf_op jit(solution)/shard_map/scatter-add | solution.py:104
  279.9 8.0 %collective-permute-done = bf16[4,128,256]{2,1,0:T(8,128)(2,1)S(1)} collective-permute-done((bf16[4,128,256]{2,1,0:T(8,128)(2,1)S(1)}, bf16[4,128,256]{2,1,0:T(8,128)(2,1)S(1)}, u32[]{:S(2)}, u32[]{:S(2)}) %collective-permute-start) | collective-permute-done | bytes 262176 | tf_op jit(solution)/shard_map/ppermute | solution.py:12
  292.8 3.5 scatter_custom_fusion.29
  296.2 9.1 %all-to-all-start.15 = ((bf16[16,48,256]{2,1,0:T(8,128)(2,1)}), bf16[16,48,256]{2,1,0:T(8,128)(2,1)S(1)}, u32[]{:S(2)}, u32[]{:S(2)}) async-start(bf16[16,48,256]{2,1,0:T(8,128)(2,1)} %bitcast.428), calls=%async_computation.15 | async-start | bytes 786432 | tf_op jit(solution)/shard_map/all_to_all | solution.py:96
  310.5 3.5 scatter_custom_fusion.25
  318.2 1.8 fusion.12
  320.7 7.2 all-to-all-start.13
  329.0 3.2 scatter_custom_fusion.17
  335.6 7.3 %scatter_custom_fusion.30 = f32[129,256]{1,0:T(8,128)} fusion(s32[768]{0:T(1024)} %copy-done.161, bf16[768,256]{1,0:T(8,128)(2,1)S(1)} %bitcast.420, f32[]{:T(128)} %constant.12.clone.1), kind=kCustom, calls=%fused_computation.90 | custom fusion | flops 393216 | bytes 525824 | tf_op jit(solution)/shard_map/scatter-add | solution.py:104
  342.9 7.1 all-to-all-start.9
  350.1 7.7 %scatter_custom_fusion.26 = f32[129,256]{1,0:T(8,128)} fusion(s32[768]{0:T(1024)} %fusion.354, bf16[768,256]{1,0:T(8,128)(2,1)} %bitcast.120, f32[]{:T(128)} %constant.12.clone.1), kind=kCustom, calls=%fused_computation.94 | custom fusion | flops 393216 | bytes 525824 | tf_op jit(solution)/shard_map/scatter-add | solution.py:104
  357.9 1.8 fusion.381
  361.7 3.2 scatter_custom_fusion.21
  364.9 7.1 all-to-all-start.11
  372.0 7.6 %scatter_custom_fusion.18 = f32[129,256]{1,0:T(8,128)} fusion(s32[768]{0:T(1024)} %copy-done.159, bf16[768,256]{1,0:T(8,128)(2,1)} %bitcast.114, f32[]{:T(128)} %constant.12.clone.1), kind=kCustom, calls=%fused_computation.102 | custom fusion | flops 393216 | bytes 525824 | tf_op jit(solution)/shard_map/scatter-add | solution.py:104
  382.5 3.5 scatter_custom_fusion.31
  391.0 7.1 all-to-all-start.16
  398.1 7.7 %scatter_custom_fusion.22 = f32[129,256]{1,0:T(8,128)} fusion(s32[768]{0:T(1024)} %fusion.352, bf16[768,256]{1,0:T(8,128)(2,1)} %bitcast.423, f32[]{:T(128)} %constant.12.clone.1), kind=kCustom, calls=%fused_computation.98 | custom fusion | flops 393216 | bytes 525824 | tf_op jit(solution)/shard_map/scatter-add | solution.py:104
  406.0 2.0 fusion.387
  417.9 3.3 scatter_custom_fusion.19
  421.7 3.2 scatter_custom_fusion.23
  425.8 7.1 all-to-all-start.10
  436.8 10.9 %all-to-all-done.10 = bf16[16,48,256]{2,1,0:T(8,128)(2,1)S(1)} async-done(((bf16[16,48,256]{2,1,0:T(8,128)(2,1)}), bf16[16,48,256]{2,1,0:T(8,128)(2,1)S(1)}, u32[]{:S(2)}, u32[]{:S(2)}) %all-to-all-start.10) | async-done | bytes 393248 | tf_op jit(solution)/shard_map/all_to_all | solution.py:96
  447.7 3.6 all-to-all-start.12
  451.5 3.4 scatter_custom_fusion.27
  454.9 6.9 scatter_custom_fusion.32
  462.6 100.3 %all-reduce = (f32[768]{0:T(1024)S(1)}, f32[8,768]{1,0:T(8,128)S(1)}) all-reduce(f32[768]{0:T(1024)S(1)} %add_add_fusion, f32[8,768]{1,0:T(8,128)S(1)} %fusion.20), channel_id=1, replica_groups=mesh['band'=32,'gate'=16] {'band','gate'}, use_global_device_ids=true, to_apply=%region_45.46 | all-reduce | flops 6912 | bytes 55296 | tf_op jit(solution)/shard_map/psum | solution.py:155
  563.6 5.7 all-to-all-start.14
  569.9 124.2 %all-reduce.3.cloned.1.call-done = f32[256,768]{0,1:T(8,128)} async-done(((f32[256,768]{0,1:T(8,128)}), f32[256,768]{0,1:T(8,128)}) %all-reduce.3.cloned.1.call-update) | async-done | bytes 786448 | tf_op jit(solution)/shard_map/psum | solution.py:155
  696.5 6.8 scatter_custom_fusion.20
  703.3 7.0 scatter_custom_fusion.24
  710.4 6.7 scatter_custom_fusion.28
  (557 shorter events, 125.4 us)
Async XLA Ops:
  7.2 42.4 %copy-start = (bf16[256,768]{1,0:T(8,128)(2,1)S(1)}, bf16[256,768]{1,0:T(8,128)(2,1)}, u32[]{:S(2)}) copy-start(bf16[256,768]{1,0:T(8,128)(2,1)} %param.15) | copy-start | bytes 1179652
  20.9 28.6 %copy-start.2 = (bf16[4,1,2,128,256]{4,3,2,1,0:T(8,128)(2,1)S(1)}, bf16[4,1,2,128,256]{4,3,2,1,0:T(8,128)(2,1)}, u32[]{:S(2)}) copy-start(bf16[4,1,2,128,256]{4,3,2,1,0:T(8,128)(2,1)} %param.9) | copy-start | bytes 1572868
  36.9 12.6 %copy-start.108 = (f32[768]{0:T(1024)S(1)}, f32[768]{0:T(1024)}, u32[]{:S(2)}) copy-start(f32[768]{0:T(1024)} %param.16) | copy-start | bytes 9220
  37.7 28.3 %all-to-all-start = ((s32[16,1,384]{2,1,0:T(1,128)}), s32[16,1,384]{2,1,0:T(1,128)S(1)}, u32[]{:S(2)}, u32[]{:S(2)}) async-start(s32[16,1,384]{2,1,0:T(1,128)} %reshape.1171), calls=%async_computation | async-start | bytes 49152 | tf_op jit(solution)/shard_map/all_to_all | solution.py:85
  50.0 8.0 %copy-start.6 = (f32[128,768]{1,0:T(8,128)}, f32[128,768]{1,0:T(8,128)S(1)}, u32[]{:S(2)}) copy-start(f32[128,768]{1,0:T(8,128)S(1)} %convolution_add_fusion.5) | copy-start | bytes 1179652
  52.9 21.0 %copy-start.163 = (s32[128]{0:T(128)}, s32[128]{0:T(128)S(1)}, u32[]{:S(2)}) copy-start(s32[128]{0:T(128)S(1)} %get-tuple-element.150) | copy-start | bytes 1540
  52.9 26.6 %copy-start.169 = (s32[128]{0:T(128)}, s32[128]{0:T(128)S(1)}, u32[]{:S(2)}) copy-start(s32[128]{0:T(128)S(1)} %get-tuple-element.144) | copy-start | bytes 1540
  52.9 27.8 %copy-start.167 = (s32[128]{0:T(128)}, s32[128]{0:T(128)S(1)}, u32[]{:S(2)}) copy-start(s32[128]{0:T(128)S(1)} %get-tuple-element.147) | copy-start | bytes 1540
  55.8 4.7 copy-start.138
  57.2 3.6 copy-start.136
  61.7 14.1 %copy-start.179 = (s32[512,1]{0,1:T(1,128)}, s32[512,1]{0,1:T(1,128)S(1)}, u32[]{:S(2)}) copy-start(s32[512,1]{0,1:T(1,128)S(1)} %get-tuple-element.136) | copy-start | bytes 6148
  66.6 21.9 %all-to-all-start.7 = ((bf16[16,48,256]{2,1,0:T(8,128)(2,1)}), bf16[16,48,256]{2,1,0:T(8,128)(2,1)}, u32[]{:S(2)}, u32[]{:S(2)}) async-start(bf16[16,48,256]{2,1,0:T(8,128)(2,1)} %bitcast.65), calls=%async_computation.7 | async-start | bytes 786432 | tf_op jit(solution)/shard_map/all_to_all | solution.py:96
  82.0 32.0 %copy-start.7 = (f32[128,768]{1,0:T(8,128)}, f32[128,768]{1,0:T(8,128)S(1)}, u32[]{:S(2)}) copy-start(f32[128,768]{1,0:T(8,128)S(1)} %convolution_add_fusion.10) | copy-start | bytes 1179652
  88.5 17.9 %all-to-all-start.1 = ((bf16[16,48,256]{2,1,0:T(8,128)(2,1)}), bf16[16,48,256]{2,1,0:T(8,128)(2,1)}, u32[]{:S(2)}, u32[]{:S(2)}) async-start(bf16[16,48,256]{2,1,0:T(8,128)(2,1)} %bitcast.424), calls=%async_computation.1 | async-start | bytes 786432 | tf_op jit(solution)/shard_map/all_to_all | solution.py:96
  98.4 8.0 %copy-start.159 = (s32[768]{0:T(1024)}, s32[768]{0:T(1024)S(1)}, u32[]{:S(2)}) copy-start(s32[768]{0:T(1024)S(1)} %fusion.350) | copy-start | bytes 9220
  116.5 36.4 %copy-start.15 = (f32[128,256]{1,0:T(8,128)}, f32[128,256]{1,0:T(8,128)S(1)}, u32[]{:S(2)}) copy-start(f32[128,256]{1,0:T(8,128)S(1)} %get-tuple-element.47) | copy-start | bytes 393220
  122.6 8.0 %copy-start.36 = (f32[8,768]{1,0:T(8,128)S(1)}, f32[8,768]{1,0:T(8,128)}, u32[]{:S(2)}) copy-start(f32[8,768]{1,0:T(8,128)} %param.17) | copy-start | bytes 73732
  122.6 21.3 %all-to-all-start.5 = ((bf16[16,48,256]{2,1,0:T(8,128)(2,1)}), bf16[16,48,256]{2,1,0:T(8,128)(2,1)}, u32[]{:S(2)}, u32[]{:S(2)}) async-start(bf16[16,48,256]{2,1,0:T(8,128)(2,1)} %bitcast.433), calls=%async_computation.5 | async-start | bytes 786432 | tf_op jit(solution)/shard_map/all_to_all | solution.py:96
  143.9 24.4 %all-to-all-start.3 = ((bf16[16,48,256]{2,1,0:T(8,128)(2,1)}), bf16[16,48,256]{2,1,0:T(8,128)(2,1)S(1)}, u32[]{:S(2)}, u32[]{:S(2)}) async-start(bf16[16,48,256]{2,1,0:T(8,128)(2,1)} %bitcast.429), calls=%async_computation.3 | async-start | bytes 786432 | tf_op jit(solution)/shard_map/all_to_all | solution.py:96
  169.1 25.8 %all-to-all-start.2 = ((bf16[16,48,256]{2,1,0:T(8,128)(2,1)}), bf16[16,48,256]{2,1,0:T(8,128)(2,1)}, u32[]{:S(2)}, u32[]{:S(2)}) async-start(bf16[16,48,256]{2,1,0:T(8,128)(2,1)} %bitcast.18), calls=%async_computation.2 | async-start | bytes 786432 | tf_op jit(solution)/shard_map/all_to_all | solution.py:96
  175.6 7.7 %copy-start.26 = (f32[128,256]{1,0:T(8,128)S(1)}, f32[128,256]{1,0:T(8,128)}, u32[]{:S(2)}) copy-start(f32[128,256]{1,0:T(8,128)} %get-tuple-element.111) | copy-start | bytes 393220
  175.6 7.7 %copy-start.29 = (f32[128,256]{1,0:T(8,128)S(1)}, f32[128,256]{1,0:T(8,128)}, u32[]{:S(2)}) copy-start(f32[128,256]{1,0:T(8,128)} %get-tuple-element.109) | copy-start | bytes 393220
  194.9 21.8 %all-to-all-start.4 = ((bf16[16,48,256]{2,1,0:T(8,128)(2,1)}), bf16[16,48,256]{2,1,0:T(8,128)(2,1)}, u32[]{:S(2)}, u32[]{:S(2)}) async-start(bf16[16,48,256]{2,1,0:T(8,128)(2,1)} %bitcast.432), calls=%async_computation.4 | async-start | bytes 786432 | tf_op jit(solution)/shard_map/all_to_all | solution.py:96
  216.7 18.9 %all-to-all-start.6 = ((bf16[16,48,256]{2,1,0:T(8,128)(2,1)}), bf16[16,48,256]{2,1,0:T(8,128)(2,1)}, u32[]{:S(2)}, u32[]{:S(2)}) async-start(bf16[16,48,256]{2,1,0:T(8,128)(2,1)} %bitcast.427), calls=%async_computation.6 | async-start | bytes 786432 | tf_op jit(solution)/shard_map/all_to_all | solution.py:96
  235.5 33.5 %all-to-all-start.8 = ((bf16[16,48,256]{2,1,0:T(8,128)(2,1)}), bf16[16,48,256]{2,1,0:T(8,128)(2,1)}, u32[]{:S(2)}, u32[]{:S(2)}) async-start(bf16[16,48,256]{2,1,0:T(8,128)(2,1)} %bitcast.431), calls=%async_computation.8 | async-start | bytes 786432 | tf_op jit(solution)/shard_map/all_to_all | solution.py:96
  241.9 27.2 %copy-start.160 = (s32[768]{0:T(1024)}, s32[768]{0:T(1024)S(1)}, u32[]{:S(2)}) copy-start(s32[768]{0:T(1024)S(1)} %fusion.355) | copy-start | bytes 9220
  277.5 10.4 %copy-start.10 = (f32[128,256]{1,0:T(8,128)S(1)}, f32[128,256]{1,0:T(8,128)}, u32[]{:S(2)}) copy-start(f32[128,256]{1,0:T(8,128)} %copy-done.9) | copy-start | bytes 393220
  277.5 10.4 %copy-start.12 = (f32[128,256]{1,0:T(8,128)S(1)}, f32[128,256]{1,0:T(8,128)}, u32[]{:S(2)}) copy-start(f32[128,256]{1,0:T(8,128)} %copy-done.11) | copy-start | bytes 393220
  277.5 10.4 %copy-start.14 = (f32[128,256]{1,0:T(8,128)S(1)}, f32[128,256]{1,0:T(8,128)}, u32[]{:S(2)}) copy-start(f32[128,256]{1,0:T(8,128)} %copy-done.13) | copy-start | bytes 393220
  277.5 10.4 %copy-start.137 = (pred[128]{0:T(512)(128)(4,1)S(1)}, pred[128]{0:T(512)(128)(4,1)}, u32[]{:S(2)}) copy-start(pred[128]{0:T(512)(128)(4,1)} %copy-done.136) | copy-start | bytes 388
  277.5 10.4 %copy-start.139 = (pred[128]{0:T(512)(128)(4,1)S(1)}, pred[128]{0:T(512)(128)(4,1)}, u32[]{:S(2)}) copy-start(pred[128]{0:T(512)(128)(4,1)} %copy-done.138) | copy-start | bytes 388
  278.5 10.3 %copy-start.49 = (f32[128,256]{1,0:T(8,128)S(1)}, f32[128,256]{1,0:T(8,128)}, u32[]{:S(2)}) copy-start(f32[128,256]{1,0:T(8,128)} %copy-done.48) | copy-start | bytes 393220
  278.5 9.4 %collective-permute-start = (bf16[4,128,256]{2,1,0:T(8,128)(2,1)S(1)}, bf16[4,128,256]{2,1,0:T(8,128)(2,1)S(1)}, u32[]{:S(2)}, u32[]{:S(2)}) collective-permute-start(bf16[4,128,256]{2,1,0:T(8,128)(2,1)S(1)} %pad_maximum_fusion), channel_id=1, source_target_pairs={{16,0},{32,16},{48,32},{64,48},{80,64},{96,80},{112,96},{128,112},... | collective-permute-start | bytes 786440 | tf_op jit(solution)/shard_map/ppermute | solution.py:12
  296.2 9.1 %copy-start.47 = (f32[128,256]{1,0:T(8,128)S(1)}, f32[128,256]{1,0:T(8,128)}, u32[]{:S(2)}) copy-start(f32[128,256]{1,0:T(8,128)} %copy-done.46) | copy-start | bytes 393220
  296.2 23.8 %all-to-all-start.15 = ((bf16[16,48,256]{2,1,0:T(8,128)(2,1)}), bf16[16,48,256]{2,1,0:T(8,128)(2,1)S(1)}, u32[]{:S(2)}, u32[]{:S(2)}) async-start(bf16[16,48,256]{2,1,0:T(8,128)(2,1)} %bitcast.428), calls=%async_computation.15 | async-start | bytes 786432 | tf_op jit(solution)/shard_map/all_to_all | solution.py:96
  310.5 3.5 copy-start.75
  310.5 3.5 copy-start.92
  310.5 3.5 copy-start.94
  320.0 8.0 %copy-start.87 = (bf16[128,256]{1,0:T(8,128)(2,1)S(1)}, bf16[128,256]{1,0:T(8,128)(2,1)}, u32[]{:S(2)}) copy-start(bf16[128,256]{1,0:T(8,128)(2,1)} %copy-done.86) | copy-start | bytes 196612
  320.7 22.2 %all-to-all-start.13 = ((bf16[16,48,256]{2,1,0:T(8,128)(2,1)}), bf16[16,48,256]{2,1,0:T(8,128)(2,1)}, u32[]{:S(2)}, u32[]{:S(2)}) async-start(bf16[16,48,256]{2,1,0:T(8,128)(2,1)} %bitcast.89), calls=%async_computation.13 | async-start | bytes 786432 | tf_op jit(solution)/shard_map/all_to_all | solution.py:96
  342.9 22.0 %all-to-all-start.9 = ((bf16[16,48,256]{2,1,0:T(8,128)(2,1)}), bf16[16,48,256]{2,1,0:T(8,128)(2,1)}, u32[]{:S(2)}, u32[]{:S(2)}) async-start(bf16[16,48,256]{2,1,0:T(8,128)(2,1)} %bitcast.422), calls=%async_computation.9 | async-start | bytes 786432 | tf_op jit(solution)/shard_map/all_to_all | solution.py:96
  350.1 7.8 %copy-start.20 = (f32[128,256]{1,0:T(8,128)S(1)}, f32[128,256]{1,0:T(8,128)}, u32[]{:S(2)}) copy-start(f32[128,256]{1,0:T(8,128)} %copy-done.17) | copy-start | bytes 393220
  350.1 7.8 %copy-start.23 = (f32[128,256]{1,0:T(8,128)S(1)}, f32[128,256]{1,0:T(8,128)}, u32[]{:S(2)}) copy-start(f32[128,256]{1,0:T(8,128)} %copy-done.21) | copy-start | bytes 393220
  350.1 7.8 %copy-start.28 = (f32[128,256]{1,0:T(8,128)S(1)}, f32[128,256]{1,0:T(8,128)}, u32[]{:S(2)}) copy-start(f32[128,256]{1,0:T(8,128)} %get-tuple-element.111) | copy-start | bytes 393220
  350.1 7.8 %copy-start.135 = (pred[128]{0:T(512)(128)(4,1)S(1)}, pred[128]{0:T(512)(128)(4,1)}, u32[]{:S(2)}) copy-start(pred[128]{0:T(512)(128)(4,1)} %copy-done.132) | copy-start | bytes 388
  364.9 25.3 %all-to-all-start.11 = ((bf16[16,48,256]{2,1,0:T(8,128)(2,1)}), bf16[16,48,256]{2,1,0:T(8,128)(2,1)S(1)}, u32[]{:S(2)}, u32[]{:S(2)}) async-start(bf16[16,48,256]{2,1,0:T(8,128)(2,1)} %bitcast.426), calls=%async_computation.11 | async-start | bytes 786432 | tf_op jit(solution)/shard_map/all_to_all | solution.py:96
  372.0 7.6 %copy-start.53 = (f32[128,256]{1,0:T(8,128)S(1)}, f32[128,256]{1,0:T(8,128)}, u32[]{:S(2)}) copy-start(f32[128,256]{1,0:T(8,128)} %get-tuple-element.110) | copy-start | bytes 393220
  382.5 3.5 copy-start.106
  391.0 34.8 %all-to-all-start.16 = ((bf16[16,48,256]{2,1,0:T(8,128)(2,1)}), bf16[16,48,256]{2,1,0:T(8,128)(2,1)S(1)}, u32[]{:S(2)}, u32[]{:S(2)}) async-start(bf16[16,48,256]{2,1,0:T(8,128)(2,1)} %bitcast.99), calls=%async_computation.16 | async-start | bytes 786432 | tf_op jit(solution)/shard_map/all_to_all | solution.py:96
  398.1 296.1 %all-reduce.3.cloned.1.call-start = ((), (), s32[]{:S(2)}) async-start(), calls=%async_computation.17 | async-start | bytes 1572864 | tf_op jit(solution)/shard_map/psum | solution.py:155
  398.1 7.8 %copy-start.16 = (f32[128,256]{1,0:T(8,128)S(1)}, f32[128,256]{1,0:T(8,128)}, u32[]{:S(2)}) copy-start(f32[128,256]{1,0:T(8,128)} %copy-done.15) | copy-start | bytes 393220
  398.1 7.8 %copy-start.25 = (f32[128,256]{1,0:T(8,128)S(1)}, f32[128,256]{1,0:T(8,128)}, u32[]{:S(2)}) copy-start(f32[128,256]{1,0:T(8,128)} %copy-done.24) | copy-start | bytes 393220
  398.1 7.8 %copy-start.141 = (pred[128]{0:T(512)(128)(4,1)S(1)}, pred[128]{0:T(512)(128)(4,1)}, u32[]{:S(2)}) copy-start(pred[128]{0:T(512)(128)(4,1)} %fusion.360) | copy-start | bytes 388
  398.1 7.8 %copy-start.145 = (pred[128]{0:T(512)(128)(4,1)S(1)}, pred[128]{0:T(512)(128)(4,1)}, u32[]{:S(2)}) copy-start(pred[128]{0:T(512)(128)(4,1)} %fusion.362) | copy-start | bytes 388
  398.1 7.8 %copy-start.156 = (pred[128]{0:T(512)(128)(4,1)S(1)}, pred[128]{0:T(512)(128)(4,1)}, u32[]{:S(2)}) copy-start(pred[128]{0:T(512)(128)(4,1)} %fusion.364) | copy-start | bytes 388
  408.2 3.7 copy-start.68
  408.2 4.0 copy-start.66
  408.2 5.1 copy-start.64
  425.8 21.9 %all-to-all-start.10 = ((bf16[16,48,256]{2,1,0:T(8,128)(2,1)}), bf16[16,48,256]{2,1,0:T(8,128)(2,1)S(1)}, u32[]{:S(2)}, u32[]{:S(2)}) async-start(bf16[16,48,256]{2,1,0:T(8,128)(2,1)} %bitcast.75), calls=%async_computation.10 | async-start | bytes 786432 | tf_op jit(solution)/shard_map/all_to_all | solution.py:96
  447.7 3.6 copy-start.130
  447.7 115.9 %all-to-all-start.12 = ((bf16[16,48,256]{2,1,0:T(8,128)(2,1)}), bf16[16,48,256]{2,1,0:T(8,128)(2,1)S(1)}, u32[]{:S(2)}, u32[]{:S(2)}) async-start(bf16[16,48,256]{2,1,0:T(8,128)(2,1)} %bitcast.83), calls=%async_computation.12 | async-start | bytes 786432 | tf_op jit(solution)/shard_map/all_to_all | solution.py:96
  454.9 6.9 copy-start.117
  454.9 6.9 copy-start.181
  563.6 146.8 %all-to-all-start.14 = ((bf16[16,48,256]{2,1,0:T(8,128)(2,1)}), bf16[16,48,256]{2,1,0:T(8,128)(2,1)S(1)}, u32[]{:S(2)}, u32[]{:S(2)}) async-start(bf16[16,48,256]{2,1,0:T(8,128)(2,1)} %bitcast.91), calls=%async_computation.14 | async-start | bytes 786432 | tf_op jit(solution)/shard_map/all_to_all | solution.py:96
  (140 other events, 179.4 us)
Sparse Core Ops, SparseCore 0:
  416.6 277.4 all-reduce.2
where the time goes:
time: 738 us; the launch traced here: 725 us
  other arithmetic  169 us (23%)
  waiting for transfers between devices  162 us (22%)
  local copies, waits for them, and re-layouts  134 us (18%)
  starting transfers between devices  113 us (15%)
  blocking collectives  100 us (14%)
  matrix products  30.2 us (4%)
  between operations  16.6 us (2%)
    psum x1, waiting for transfers between devices, shards(): lax.psum((weight_total, bias_total, table_total), ('band', 'gate'))  124 us
    scatter-add x16, other arithmetic, deliver(): fanin_grad.at[arrived[circuit, level].reshape(-1)]  118 us
    psum x1, blocking collectives, shards(): lax.psum((weight_total, bias_total, table_total), ('band', 'gate'))  100 us
    all_to_all x16, starting transfers between devices, deliver(): lax.all_to_all(sending.reshape(groups, slot_cap, hidden), 'gate', split_a...  99.6 us
    scatter x16, local copies, waits for them, and re-layouts, deliver(): sending.at[offsets[circuit, level]]  54.6 us
    all_to_all x16, waiting for transfers between devices, deliver(): lax.all_to_all(sending.reshape(groups, slot_cap, hidden), 'gate', split_a...  30.1 us
    unnamed x375, local copies, waits for them, and re-layouts  30.1 us
    another operation x22, other arithmetic  28.8 us
  transfers between devices with their start and end apart: 19, of which 6 were waited for; matrix products, arithmetic and copies ran while one was open for 33% of the time, Pallas kernels for 0%

commit v1 on v0

v1 whole, which is shorter than its diff:
```python
import math

import jax
import jax.numpy as jnp
from jax import lax
from jax.experimental import pallas as pl
from jax.experimental.pallas import tpu as pltpu
from jax.sharding import PartitionSpec as P

F32 = jnp.float32
BF16 = jnp.bfloat16
H = 256
ROWS = 128
GATES = 16
CIRC = 4
OWN = 1024
CHUNK = 256
NCH = OWN // CHUNK
SHARE = 896


def iota(shape, dim):
    return lax.broadcasted_iota(jnp.int32, shape, dim)


def dot_tn(a, b):
    return lax.dot_general(a, b, (((0,), (0,)), ((), ())), preferred_element_type=F32)


def dot_nt(a, b):
    return lax.dot_general(a, b, (((1,), (1,)), ((), ())), preferred_element_type=F32)


def dot_nn(a, b):
    return jnp.dot(a, b, preferred_element_type=F32)


def kernel_body(
    bands,
    cols,
    msg,
    types,
    sg,
    owner,
    slot,
    live,
    w,
    bias,
    table,
    out,
    wout,
    eout,
    idx_s,
    idx_r,
    pieces,
    m0,
    sg0,
    m1,
    dm_s,
    d1,
    d2,
    d3,
    d4,
    sel,
    coef,
    xts,
    s0,
    gbuf,
    q_s,
    q_r,
    wacc,
    eacc,
    wsend0,
    wsend1,
    wr0,
    wr1,
    ysend,
    yr,
    xsend,
    xr,
    ag,
    sem_s,
    idx_sem,
    m0_sem,
    sg0_sem,
    dm_sem,
    m1_sem,
    fw_sem,
    ex_sem,
    q_sem,
    out_sem,
    wr_sem,
):
    rows_y = cols
    rows_x = bands // cols
    me = lax.axis_index("gate")
    band = lax.axis_index("band")
    z = me // 2
    half = lax.rem(me, 2)
    active = lax.rem(z, 2) == 0
    mine = z // 2
    sibling = me + 1 - 2 * half
    by = lax.rem(band, rows_y)
    bx = band // rows_y

    def send(src, dst, ssem, rsem, gate=None, to_band=None):
        where = {}
        if to_band is not None:
            where["band"] = to_band
        if gate is not None:
            where["gate"] = gate
        pltpu.make_async_remote_copy(
            src_ref=src,
            dst_ref=dst,
            send_sem=ssem,
            recv_sem=rsem,
            device_id=where,
            device_id_type=pl.DeviceIdType.MESH,
        ).start()

    def wait(ref, sem):
        pltpu.make_async_copy(ref, ref, sem).wait()

    def each(count, body):
        def step(i, carry):
            body(i)
            return carry

        lax.fori_loop(0, count, step, 0)

    barrier = pltpu.get_barrier_semaphore()

    def greet(**where):
        pl.semaphore_signal(
            barrier, inc=1, device_id=where, device_id_type=pl.DeviceIdType.MESH
        )

    each(GATES - 1, lambda i: greet(gate=lax.rem(me + 1 + i, GATES)))
    each(rows_y - 1, lambda i: greet(band=bx * rows_y + lax.rem(by + 1 + i, rows_y)))
    if rows_x > 1:
        each(rows_x - 1, lambda i: greet(band=lax.rem(bx + 1 + i, rows_x) * rows_y + by))
    greet(band=lax.rem(band + 1, bands))
    greet(band=lax.rem(band + bands - 1, bands))

    for c in range(CIRC):
        for lv in range(2):
            idx_s[c, 4 * lv : 4 * lv + 4, :] = owner[c, lv] * ROWS + slot[c, lv]
        idx_s[c, 8:10, :] = types[c]
        idx_s[c, 10:16, :] = jnp.zeros((6, ROWS), jnp.int32)
    full = table[...] + jnp.where(iota((8, 3 * H), 1) < 2 * H, bias[...], 0.0)
    hi = full.astype(BF16)
    rest = full - hi.astype(F32)
    mid = rest.astype(BF16)
    low = (rest - mid.astype(F32)).astype(BF16)
    pieces[...] = jnp.concatenate(
        [hi.astype(F32), mid.astype(F32), low.astype(F32), jnp.zeros((8, 3 * H), F32)], axis=0
    ).astype(BF16)
    cand_bias = bias[:, 2 * H :]

    pl.semaphore_wait(barrier, GATES - 1 + rows_y - 1 + rows_x - 1 + 2)

    def to_task(src_of, dst, ssem, rsem):
        for c in range(CIRC):
            local = jnp.logical_and(active, mine == c)

            @pl.when(local)
            def _():
                dst[...] = src_of(c)[...]

            @pl.when(jnp.logical_not(local))
            def _():
                send(src_of(c), dst, ssem, rsem, gate=4 * c + half)

    for c in range(CIRC):
        for h in range(2):
            local = me == 4 * c + h

            @pl.when(local)
            def _():
                idx_r[me] = idx_s[c]

            @pl.when(jnp.logical_not(local))
            def _():
                send(idx_s.at[c], idx_r.at[me], sem_s.at[0], idx_sem, gate=4 * c + h)

    zrows = pl.ds(pl.multiple_of(z * ROWS, ROWS), ROWS)
    to_task(lambda c: msg.at[c, 0], m0.at[zrows], sem_s.at[1], m0_sem.at[z])
    to_task(lambda c: sg.at[c, 0], sg0.at[zrows], sem_s.at[2], sg0_sem)

    def coefficients(m, kinds, gate0, count):
        hot = jnp.where(lax.bitwise_and(iota((32, ROWS), 0), 7) == kinds, 1.0, 0.0).astype(BF16)
        inp = dot_tn(hot, pieces[...])
        pre = dot_nn(m, w[...])
        tr = jnp.tanh(0.5 * (inp[:, :H] + pre[:, :H]))
        tu = jnp.tanh(0.5 * (inp[:, H : 2 * H] + pre[:, H : 2 * H]))
        cand = pre[:, 2 * H :] + cand_bias
        r = 0.5 + 0.5 * tr
        u = 0.5 + 0.5 * tu
        new = jnp.tanh(inp[:, 2 * H :] + r * cand)
        on = jnp.where(iota((ROWS, 1), 0) + gate0 < count, 1.0, 0.0)
        a = (1.0 - u) * (1.0 - new * new) * on
        dc = a * r
        dr = a * cand * (r * (1.0 - r))
        dz = (m.astype(F32) - new) * (u * (1.0 - u)) * on
        return a, dr, dz, dc, u * on

    def kinds_ext(kinds):
        row = iota((16, ROWS), 0)
        return jnp.where(jnp.logical_or(row == kinds, row == 8), 1.0, 0.0).astype(BF16)

    def grads(s, factors):
        a, b, c, d, u = factors
        dr = (s * b).astype(BF16)
        dz = (s * c).astype(BF16)
        dc = (s * d).astype(BF16)
        dn = (s * a).astype(BF16)
        down = (
            s * u
            + dot_nt(dr, w[:, :H])
            + dot_nt(dz, w[:, H : 2 * H])
            + dot_nt(dc, w[:, 2 * H :])
        )
        return dr, dz, dc, dn, down.astype(BF16)

    wacc[...] = jnp.zeros_like(wacc)
    eacc[...] = jnp.zeros_like(eacc)

    def level_one(c):
        m = msg[c, 1]
        kinds = types[c, 1:2, :]
        factors = coefficients(m, kinds, me * ROWS, live[c, 1])
        dr, dz, dc, dn, down = grads(sg[c, 1].astype(F32), factors)
        dm_s[c] = down
        ext = kinds_ext(kinds)
        for i, g in enumerate((dr, dz, dc)):
            wacc[:, i * H : (i + 1) * H] += dot_tn(m, g)
        for i, g in enumerate((dr, dz, dc, dn)):
            eacc[:, i * H : (i + 1) * H] += dot_nn(ext, g)

    each(CIRC, level_one)

    own_rows = pl.ds(pl.multiple_of(half * OWN + z * ROWS, ROWS), ROWS)
    to_task(lambda c: dm_s.at[c], d1.at[own_rows], sem_s.at[3], dm_sem.at[z])
    to_task(lambda c: msg.at[c, 1], m1.at[zrows], sem_s.at[4], m1_sem.at[z])

    def pack_shares(dst):
        for i in range(GATES):
            dst[i, :, : 3 * H] = wacc[16 * i : 16 * i + 16, :].astype(BF16)
            if i < 8:
                dst[i, :, 3 * H :] = eacc[:, ROWS * i : ROWS * (i + 1)].astype(BF16)
            else:
                dst[i, :, 3 * H :] = jnp.zeros((16, ROWS), BF16)

    def scatter_shares(src, dst, place, ssem, rsem):
        def to(i):
            peer = lax.rem(me + 1 + i, GATES)
            send(src.at[peer], dst.at[place], ssem, rsem, gate=peer)

        each(GATES - 1, to)
        dst[place] = src[me]

    pack_shares(wsend0)
    scatter_shares(wsend0, wr0, me, sem_s.at[5], wr_sem.at[0])

    def turn(t):
        off = jnp.where(lax.rem(t, 2) == 1, (t + 1) // 2, 8 - t // 2)
        return lax.rem(z + off, 8)

    @pl.when(active)
    def _():
        wait(idx_r.at[0 : GATES - 1], idx_sem)

        def build(j):
            tile = idx_r[j]
            col = pl.ds(pl.multiple_of(lax.rem(j, 2) * OWN + (j // 2) * ROWS, ROWS), ROWS)
            spot = iota((ROWS, ROWS), 0)
            block = 2 * iota((8, ROWS), 0) + half
            for lv in (1, 0):
                at = jnp.full((8, ROWS), -1, jnp.int32)
                for f in range(4):
                    t = tile[4 * lv + f : 4 * lv + f + 1, :]
                    at = jnp.where(
                        lax.shift_right_logical(t, 7) == block, lax.bitwise_and(t, 127), at
                    )
                for k in range(8):
                    sel[lv, k * ROWS : (k + 1) * ROWS, col] = jnp.where(
                        spot == at[k : k + 1, :], 1.0, 0.0
                    ).astype(BF16)

        each(GATES, build)

        def forward(lv, m_ref, sem):
            def step(t):
                k = turn(t)

                @pl.when(t > 0)
                def _():
                    wait(m_ref.at[0:ROWS], sem.at[k])

                rows = pl.ds(pl.multiple_of(k * ROWS, ROWS), ROWS)
                j = 2 * k + half
                kinds = idx_r[j, 8 + lv : 9 + lv, :]
                factors = coefficients(m_ref[rows], kinds, j * ROWS, live[mine, lv])
                for i, f in enumerate(factors):
                    coef[lv, i, rows] = f
                xts[lv, :, rows] = kinds_ext(kinds)

            each(8, step)

        forward(0, m0, m0_sem)

        def relay(t):
            k = turn(t)
            rows = pl.ds(pl.multiple_of(half * OWN + k * ROWS, ROWS), ROWS)

            @pl.when(t > 0)
            def _():
                wait(d1.at[0:ROWS], dm_sem.at[k])

            send(d1.at[rows], d1.at[rows], sem_s.at[6], fw_sem, gate=sibling)

        each(8, relay)
        wait(sg0.at[0 : 7 * ROWS], sg0_sem)
        wait(d1.at[0:OWN], fw_sem)

        def chunk(n):
            return pl.ds(pl.multiple_of(n * CHUNK, CHUNK), CHUNK)

        def backward(lv, s, n, dst, sem, ssem):
            rows = chunk(n)
            factors = tuple(coef[lv, i, rows] for i in range(5))
            dr, dz, dc, dn, down = grads(s, factors)
            for i, g in enumerate((dr, dz, dc, dn)):
                gbuf[rows, i * H : (i + 1) * H] = g
            place = pl.ds(pl.multiple_of(half * OWN + n * CHUNK, CHUNK), CHUNK)
            dst[place] = down
            send(dst.at[place], dst.at[place], ssem, sem, gate=sibling)

        def collect(lv, n, src):
            return dot_nn(sel[lv, chunk(n)], src[...])

        def first_zero(n):
            s = sg0[chunk(n)].astype(F32) + collect(1, n, d1)
            s0[chunk(n)] = s
            backward(0, s, n, d2, ex_sem.at[0], sem_s.at[7])

        each(NCH, first_zero)
        wait(d2.at[0:OWN], ex_sem.at[0])

        def first_out(n):
            rows = chunk(n)
            q_s[rows] = collect(0, n, d2).astype(BF16)

            @pl.when(band > 0)
            def _():
                send(
                    q_s.at[rows],
                    q_r.at[rows],
                    sem_s.at[8],
                    q_sem.at[n],
                    to_band=jnp.maximum(band - 1, 0),
                )

            @pl.when(band == bands - 1)
            def _():
                q_r[rows] = jnp.zeros((CHUNK, H), BF16)

        each(NCH, first_out)
        forward(1, m1, m1_sem)

        def second_one(n):
            @pl.when(band < bands - 1)
            def _():
                wait(q_r.at[0:CHUNK], q_sem.at[n])

            backward(1, q_r[chunk(n)].astype(F32), n, d3, ex_sem.at[1], sem_s.at[9])

        each(NCH, second_one)

        for i in range(3):
            wacc[:, i * H : (i + 1) * H] = dot_tn(m1[...], gbuf[:, i * H : (i + 1) * H])
        for i in range(4):
            eacc[:, i * H : (i + 1) * H] = dot_nn(xts[1], gbuf[:, i * H : (i + 1) * H])
        wait(d3.at[0:OWN], ex_sem.at[1])

        def second_zero(n):
            s = s0[chunk(n)] + collect(1, n, d3)
            backward(0, s, n, d4, ex_sem.at[2], sem_s.at[10])

        each(NCH, second_zero)
        for i in range(3):
            wacc[:, i * H : (i + 1) * H] += dot_tn(m0[...], gbuf[:, i * H : (i + 1) * H])
        for i in range(4):
            eacc[:, i * H : (i + 1) * H] += dot_nn(xts[0], gbuf[:, i * H : (i + 1) * H])
        pack_shares(wsend1)
        scatter_shares(wsend1, wr1, 2 * mine + half, sem_s.at[11], wr_sem.at[1])

        wait(d4.at[0:OWN], ex_sem.at[2])

        @pl.when(band > 0)
        def _():
            wait(q_s, sem_s.at[8])

        def second_out(n):
            rows = chunk(n)
            q_s[rows] = collect(0, n, d4).astype(BF16)
            for e in range(2):
                k = 2 * n + e
                part = pl.ds(pl.multiple_of(k * ROWS, ROWS), ROWS)

                @pl.when(k == z)
                def _():
                    out[mine] = q_s[part]

                @pl.when(k != z)
                def _():
                    send(q_s.at[part], out.at[mine], sem_s.at[12], out_sem, gate=2 * k + half)

        each(NCH, second_out)

    wait(wr0.at[0 : GATES - 1], wr_sem.at[0])

    @pl.when(active)
    def _():
        wait(wr1.at[0:7], wr_sem.at[1])

    @pl.when(jnp.logical_not(active))
    def _():
        wait(wr1, wr_sem.at[1])

    total = wr0[0].astype(F32)
    for i in range(1, GATES):
        total = total + wr0[i].astype(F32)
    for i in range(8):
        total = total + wr1[i].astype(F32)
    ysend[...] = total.astype(BF16)

    def to_y(i):
        peer = bx * rows_y + lax.rem(by + 1 + i, rows_y)
        send(ysend, yr.at[by], sem_s.at[13], wr_sem.at[2], to_band=peer)

    each(rows_y - 1, to_y)
    yr[by] = ysend[...]
    wait(yr.at[0 : rows_y - 1], wr_sem.at[2])
    total = yr[0].astype(F32)
    for i in range(1, rows_y):
        total = total + yr[i].astype(F32)
    if rows_x > 1:
        xsend[...] = total.astype(BF16)

        def to_x(i):
            peer = lax.rem(bx + 1 + i, rows_x) * rows_y + by
            send(xsend, xr.at[bx], sem_s.at[14], wr_sem.at[3], to_band=peer)

        each(rows_x - 1, to_x)
        xr[bx] = xsend[...]
        wait(xr.at[0 : rows_x - 1], wr_sem.at[3])
        total = xr[0].astype(F32)
        for i in range(1, rows_x):
            total = total + xr[i].astype(F32)
    total = total * (1.0 / math.sqrt(CIRC * bands * 2 * ROWS * GATES))
    ag[me] = total.astype(BF16)

    def to_all(i):
        peer = lax.rem(me + 1 + i, GATES)
        send(ag.at[me], ag.at[me], sem_s.at[15], wr_sem.at[4], gate=peer)

    each(GATES - 1, to_all)
    wait(ag.at[0 : GATES - 1], wr_sem.at[4])
    for i in range(GATES):
        wout[16 * i : 16 * i + 16, :] = ag[i, :, : 3 * H].astype(F32)
        if i < 8:
            eout[:, ROWS * i : ROWS * (i + 1)] = ag[i, :, 3 * H :].astype(F32)

    @pl.when(active)
    def _():
        wait(out.at[0:3], out_sem)
        wait(idx_r.at[0:7], sem_s.at[0])
        for i in range(1, 5):
            wait(m0.at[0 : 3 * ROWS], sem_s.at[i])
        wait(d1.at[0:OWN], sem_s.at[6])
        wait(d1.at[0:OWN], sem_s.at[7])
        wait(d1.at[0:OWN], sem_s.at[9])
        wait(d1.at[0:OWN], sem_s.at[10])
        wait(wr0.at[0 : GATES - 1], sem_s.at[11])
        wait(q_s.at[0 : 7 * ROWS], sem_s.at[12])

    @pl.when(jnp.logical_not(active))
    def _():
        wait(out, out_sem)
        wait(idx_r.at[0:8], sem_s.at[0])
        for i in range(1, 5):
            wait(m0.at[0 : 4 * ROWS], sem_s.at[i])

    wait(wr0.at[0 : GATES - 1], sem_s.at[5])
    wait(yr.at[0 : rows_y - 1], sem_s.at[13])
    if rows_x > 1:
        wait(xr.at[0 : rows_x - 1], sem_s.at[14])
    wait(ag.at[0 : GATES - 1], sem_s.at[15])


def shards(
    messages,
    gate_type,
    state_grad,
    fanin_owner,
    fanin_slot,
    live_count,
    hidden_weight,
    hidden_bias,
    type_table,
):
    bands = lax.axis_size("band")
    cols = min(8, bands)
    owners = jnp.swapaxes(fanin_owner[:, 0], 2, 3)
    slots = jnp.swapaxes(fanin_slot[:, 0], 2, 3)
    vmem = pl.BlockSpec(memory_space=pltpu.VMEM)
    dma = pltpu.SemaphoreType.DMA

    def body(*refs):
        kernel_body(bands, cols, *refs)

    out, weight, ext = pl.pallas_call(
        body,
        out_shape=(
            jax.ShapeDtypeStruct((CIRC, ROWS, H), BF16),
            jax.ShapeDtypeStruct((H, 3 * H), F32),
            jax.ShapeDtypeStruct((16, 4 * H), F32),
        ),
        in_specs=[vmem] * 5 + [pl.BlockSpec(memory_space=pltpu.SMEM)] + [vmem] * 3,
        out_specs=(vmem, vmem, vmem),
        scratch_shapes=[
            pltpu.VMEM((CIRC, 16, ROWS), jnp.int32),
            pltpu.VMEM((GATES, 16, ROWS), jnp.int32),
            pltpu.VMEM((32, 3 * H), BF16),
            pltpu.VMEM((OWN, H), BF16),
            pltpu.VMEM((OWN, H), BF16),
            pltpu.VMEM((OWN, H), BF16),
            pltpu.VMEM((CIRC, ROWS, H), BF16),
            pltpu.VMEM((2 * OWN, H), BF16),
            pltpu.VMEM((2 * OWN, H), BF16),
            pltpu.VMEM((2 * OWN, H), BF16),
            pltpu.VMEM((2 * OWN, H), BF16),
            pltpu.VMEM((2, OWN, 2 * OWN), BF16),
            pltpu.VMEM((2, 5, OWN, H), F32),
            pltpu.VMEM((2, 16, OWN), BF16),
            pltpu.VMEM((OWN, H), F32),
            pltpu.VMEM((OWN, 4 * H), BF16),
            pltpu.VMEM((OWN, H), BF16),
            pltpu.VMEM((OWN, H), BF16),
            pltpu.VMEM((H, 3 * H), F32),
            pltpu.VMEM((16, 4 * H), F32),
            pltpu.VMEM((GATES, 16, SHARE), BF16),
            pltpu.VMEM((GATES, 16, SHARE), BF16),
            pltpu.VMEM((GATES, 16, SHARE), BF16),
            pltpu.VMEM((8, 16, SHARE), BF16),
            pltpu.VMEM((16, SHARE), BF16),
            pltpu.VMEM((cols, 16, SHARE), BF16),
            pltpu.VMEM((16, SHARE), BF16),
            pltpu.VMEM((max(bands // cols, 1), 16, SHARE), BF16),
            pltpu.VMEM((GATES, 16, SHARE), BF16),
            dma((16,)),
            dma,
            dma((8,)),
            dma,
            dma((8,)),
            dma((8,)),
            dma,
            dma((3,)),
            dma((NCH,)),
            dma,
            dma((5,)),
        ],
        compiler_params=pltpu.CompilerParams(
            collective_id=0, has_side_effects=True, vmem_limit_bytes=56 * 1024 * 1024
        ),
        name="band_passes",
    )(
        messages[:, 0],
        gate_type[:, 0],
        state_grad[:, 0],
        owners,
        slots,
        live_count[:, 0],
        hidden_weight,
        hidden_bias.reshape(1, 3 * H),
        type_table,
    )
    bias = ext[8, : 3 * H]
    rows = jnp.concatenate([ext[:8, : 2 * H], ext[:8, 3 * H :]], axis=1)
    return out[:, None], weight, bias, rows


def solution(mesh):
    return jax.shard_map(
        shards,
        mesh=mesh,
        in_specs=(
            P(None, "band", None, "gate", None),
            P(None, "band", None, "gate"),
            P(None, "band", None, "gate", None),
            P(None, "band", None, "gate", None),
            P(None, "band", None, "gate", None),
            P(None, "band", None),
            P(),
            P(),
            P(),
        ),
        out_specs=(P(None, "band", "gate", None), P(), P(), P()),
        check_vma=False,
    )
```

time: 738 us -> 129 us (0.17); the launches traced: 725 us -> 128 us
  other arithmetic: 169 us -> 0.61 us
  waiting for transfers between devices: 162 us -> 0 us
  local copies, waits for them, and re-layouts: 134 us -> 8.41 us
  Pallas kernels: 0 us -> 118 us
  starting transfers between devices: 113 us -> 0 us
  blocking collectives: 100 us -> 0 us
  matrix products: 30.2 us -> 0 us
  between operations: 16.6 us -> 0.66 us
    psum x1 -> x0, waiting for transfers between devices: 124 us -> none  [shards(): lax.psum((weight_total, bias_total, table_total), ('band', 'gate'))]
    pallas_call x0 -> x1, Pallas kernels: none -> 118 us  [shards(): pl.pallas_call(body, out_shape=(jax.ShapeDtypeStruct((CIRC, ROWS, H), BF1...]
    scatter-add x16 -> x0, other arithmetic: 118 us -> none  [deliver(): fanin_grad.at[arrived[circuit, level].reshape(-1)]]
    all_to_all x17 -> x0, starting transfers between devices: 111 us -> none  [the longest x16 99.6 us: deliver(): lax.all_to_all(sending.reshape(groups, slot_cap, hidden), 'gate', split_a...]
    psum x1 -> x0, blocking collectives: 100 us -> none  [shards(): lax.psum((weight_total, bias_total, table_total), ('band', 'gate'))]
    scatter x17 -> x0, local copies, waits for them, and re-layouts: 70.2 us -> none  [the longest x16 54.6 us: deliver(): sending.at[offsets[circuit, level]]]
    dot_general x48 -> x0, matrix products: 30.2 us -> none  [the longest x16 9.91 us: cell_backward(): lax.dot_general(grad_acts, weight, (((1,), (1,)), ((), ())), preferred_el...]
    all_to_all x17 -> x0, waiting for transfers between devices: 30.1 us -> none  [the longest x16 30.1 us: deliver(): lax.all_to_all(sending.reshape(groups, slot_cap, hidden), 'gate', split_a...]
  transfers between devices with their start and end apart: 19 -> 0, of which waited for: 6 -> 0; matrix products, arithmetic and copies ran while one was open for 33% -> 0% of each run, Pallas kernels for 0% -> 0%
where the time goes in v1:
time: 129 us; the launch traced here: 128 us
  Pallas kernels  118 us (91%)
  local copies, waits for them, and re-layouts  8.41 us (7%)
    pallas_call x1, Pallas kernels, shards(): pl.pallas_call(body, out_shape=(jax.ShapeDtypeStruct((CIRC, ROWS, H), BF1...  118 us
    unnamed x6, local copies, waits for them, and re-layouts  4.41 us

profile of v1, /device:TPU:1, one launch (start us, length us, event | category | flops | bytes accessed | tf_op | source)
XLA Modules:
  0.0 127.7 jit_solution(9493949941358907064)
XLA Ops:
  0.6 0.0 copy-start
  0.6 0.0 copy-start.1
  0.7 0.7 copy-done.1
  1.3 0.7 copy.13.refs_5_
  2.0 0.0 copy-done
  2.0 0.6 reshape.11.refs_7_
  2.6 118.0 %band_passes.1 = (bf16[4,128,256]{2,1,0:T(8,128)(2,1)}, f32[256,768]{1,0:T(8,128)}, f32[16,1024]{1,0:T(8,128)}) custom-call(bf16[4,2,128,256]{3,2,1,0:T(8,128)(2,1)} %bitcast.13, s32[4,2,128]{2,1,0:T(2,128)} %bitcast.18, bf16[4,2,128,256]{3,2,1,0:T(8,128)(2,1)} %bitcast.14, s32[4,2,4,128]{3,2,1,0:T(4,128)} %bitcast.16, s32[4,2,4,128]{3,2,1,0:T(4,128)} %bitcast.17, ...), custom_call_target="tpu_custom_call" | custom-call | tf_op jit(solution)/shard_map/band_passes/pallas_call | solution.py:523
  120.6 1.3 %slice_reduce_fusion = f32[768]{0:T(1024)} fusion(f32[16,1024]{1,0:T(8,128)} %get-tuple-element.9), kind=kLoop, calls=%fused_computation.1 | loop fusion | bytes 6144 | tf_op jit(solution)/shard_map/slice | solution.py:589
  121.9 0.7 slice.11
  122.6 0.7 slice.10
  123.3 0.6 pad_maximum_fusion
  123.9 1.7 %copy.17 = bf16[4,1,128,256]{3,2,1,0:T(8,128)(2,1)} copy(bf16[4,1,128,256]{3,2,1,0:T(8,128)(2,1)} %bitcast.15) | data formatting | bytes 524288
  125.6 2.1 %copy.18 = f32[256,768]{1,0:T(8,128)} copy(f32[256,768]{1,0:T(8,128)} %get-tuple-element.19) | data formatting | bytes 1572864
Async XLA Ops:
  0.6 1.4 %copy-start = (f32[768]{0:T(1024)S(1)}, f32[768]{0:T(1024)}, u32[]{:S(2)}) copy-start(f32[768]{0:T(1024)} %param.16) | copy-start | bytes 9220
  0.6 0.7 copy-start.1

commit v2 on v1

--- a/solution.py
+++ b/solution.py
@@ -16,7 +16,7 @@
 OWN = 1024
 CHUNK = 256
 NCH = OWN // CHUNK
-SHARE = 896
+PIECES = (8, 4, 16, H)
 
 
 def iota(shape, dim):
@@ -48,8 +48,7 @@
     bias,
     table,
     out,
-    wout,
-    eout,
+    summed,
     idx_s,
     idx_r,
     pieces,
@@ -70,15 +69,11 @@
     q_r,
     wacc,
     eacc,
-    wsend0,
-    wsend1,
-    wr0,
-    wr1,
-    ysend,
-    yr,
-    xsend,
-    xr,
-    ag,
+    half_s,
+    half_r,
+    plane_s,
+    plane_r,
+    z_r,
     sem_s,
     idx_sem,
     m0_sem,
@@ -90,6 +85,7 @@
     q_sem,
     out_sem,
     wr_sem,
+    plane_ready,
 ):
     rows_y = cols
     rows_x = bands // cols
@@ -147,7 +143,8 @@
             idx_s[c, 4 * lv : 4 * lv + 4, :] = owner[c, lv] * ROWS + slot[c, lv]
         idx_s[c, 8:10, :] = types[c]
         idx_s[c, 10:16, :] = jnp.zeros((6, ROWS), jnp.int32)
-    full = table[...] + jnp.where(iota((8, 3 * H), 1) < 2 * H, bias[...], 0.0)
+    full_bias = bias[...].reshape(1, 3 * H)
+    full = table[...] + jnp.where(iota((8, 3 * H), 1) < 2 * H, full_bias, 0.0)
     hi = full.astype(BF16)
     rest = full - hi.astype(F32)
     mid = rest.astype(BF16)
@@ -155,37 +152,7 @@
     pieces[...] = jnp.concatenate(
         [hi.astype(F32), mid.astype(F32), low.astype(F32), jnp.zeros((8, 3 * H), F32)], axis=0
     ).astype(BF16)
-    cand_bias = bias[:, 2 * H :]
-
-    pl.semaphore_wait(barrier, GATES - 1 + rows_y - 1 + rows_x - 1 + 2)
-
-    def to_task(src_of, dst, ssem, rsem):
-        for c in range(CIRC):
-            local = jnp.logical_and(active, mine == c)
-
-            @pl.when(local)
-            def _():
-                dst[...] = src_of(c)[...]
-
-            @pl.when(jnp.logical_not(local))
-            def _():
-                send(src_of(c), dst, ssem, rsem, gate=4 * c + half)
-
-    for c in range(CIRC):
-        for h in range(2):
-            local = me == 4 * c + h
-
-            @pl.when(local)
-            def _():
-                idx_r[me] = idx_s[c]
-
-            @pl.when(jnp.logical_not(local))
-            def _():
-                send(idx_s.at[c], idx_r.at[me], sem_s.at[0], idx_sem, gate=4 * c + h)
-
-    zrows = pl.ds(pl.multiple_of(z * ROWS, ROWS), ROWS)
-    to_task(lambda c: msg.at[c, 0], m0.at[zrows], sem_s.at[1], m0_sem.at[z])
-    to_task(lambda c: sg.at[c, 0], sg0.at[zrows], sem_s.at[2], sg0_sem)
+    cand_bias = full_bias[:, 2 * H :]
 
     def coefficients(m, kinds, gate0, count):
         hot = jnp.where(lax.bitwise_and(iota((32, ROWS), 0), 7) == kinds, 1.0, 0.0).astype(BF16)
@@ -228,7 +195,7 @@
     def level_one(c):
         m = msg[c, 1]
         kinds = types[c, 1:2, :]
-        factors = coefficients(m, kinds, me * ROWS, live[c, 1])
+        factors = coefficients(m, kinds, me * ROWS, live[1, c])
         dr, dz, dc, dn, down = grads(sg[c, 1].astype(F32), factors)
         dm_s[c] = down
         ext = kinds_ext(kinds)
@@ -239,28 +206,90 @@
 
     each(CIRC, level_one)
 
+    pl.semaphore_wait(barrier, GATES - 1 + rows_y - 1 + rows_x - 1 + 2)
+    each(
+        rows_x - 1,
+        lambda i: pl.semaphore_signal(
+            plane_ready,
+            inc=1,
+            device_id={"band": lax.rem(bx + 1 + i, rows_x) * rows_y + by},
+            device_id_type=pl.DeviceIdType.MESH,
+        ),
+    )
+
+    def to_task(src_of, dst, ssem, rsem):
+        for c in range(CIRC):
+            local = jnp.logical_and(active, mine == c)
+
+            @pl.when(local)
+            def _():
+                dst[...] = src_of(c)[...]
+
+            @pl.when(jnp.logical_not(local))
+            def _():
+                send(src_of(c), dst, ssem, rsem, gate=4 * c + half)
+
+    for c in range(CIRC):
+        for h in range(2):
+            local = me == 4 * c + h
+
+            @pl.when(local)
+            def _():
+                idx_r[me] = idx_s[c]
+
+            @pl.when(jnp.logical_not(local))
+            def _():
+                send(idx_s.at[c], idx_r.at[me], sem_s.at[0], idx_sem, gate=4 * c + h)
+
+    zrows = pl.ds(pl.multiple_of(z * ROWS, ROWS), ROWS)
+    to_task(lambda c: msg.at[c, 0], m0.at[zrows], sem_s.at[1], m0_sem.at[z])
+    to_task(lambda c: sg.at[c, 0], sg0.at[zrows], sem_s.at[2], sg0_sem)
+
     own_rows = pl.ds(pl.multiple_of(half * OWN + z * ROWS, ROWS), ROWS)
     to_task(lambda c: dm_s.at[c], d1.at[own_rows], sem_s.at[3], dm_sem.at[z])
-    to_task(lambda c: msg.at[c, 1], m1.at[zrows], sem_s.at[4], m1_sem.at[z])
-
-    def pack_shares(dst):
+    py, px = 8 // rows_y, 4 // rows_x
+
+    def piece_of(ref, to):
+        return ref.at[pl.ds(lax.rem(to, rows_y) * py, py), pl.ds((to // rows_y) * px, px)]
+
+    def halve(stage, ssem):
         for i in range(GATES):
-            dst[i, :, : 3 * H] = wacc[16 * i : 16 * i + 16, :].astype(BF16)
-            if i < 8:
-                dst[i, :, 3 * H :] = eacc[:, ROWS * i : ROWS * (i + 1)].astype(BF16)
+            for n in range(3):
+                half_s[stage, i % 2, i // 2, n] = wacc[
+                    16 * i : 16 * i + 16, n * H : (n + 1) * H
+                ].astype(BF16)
+            if i < 4:
+                half_s[stage, i % 2, i // 2, 3] = eacc[:, i * H : (i + 1) * H].astype(BF16)
             else:
-                dst[i, :, 3 * H :] = jnp.zeros((16, ROWS), BF16)
-
-    def scatter_shares(src, dst, place, ssem, rsem):
+                half_s[stage, i % 2, i // 2, 3] = jnp.zeros((16, H), BF16)
+        send(
+            half_s.at[stage, 1 - half], half_r.at[stage], ssem, wr_sem.at[2 * stage], gate=sibling
+        )
+
+    def over_plane(stage, ssem):
+        wait(half_r.at[stage], wr_sem.at[2 * stage])
+        for p in range(8):
+            plane_s[stage, p] = (
+                half_s[stage, half, p].astype(F32) + half_r[stage, p].astype(F32)
+            ).astype(BF16)
+
         def to(i):
-            peer = lax.rem(me + 1 + i, GATES)
-            send(src.at[peer], dst.at[place], ssem, rsem, gate=peer)
-
-        each(GATES - 1, to)
-        dst[place] = src[me]
-
-    pack_shares(wsend0)
-    scatter_shares(wsend0, wr0, me, sem_s.at[5], wr_sem.at[0])
+            peer = lax.rem(band + 1 + i, bands)
+            send(
+                piece_of(plane_s.at[stage], peer),
+                plane_r.at[stage, band],
+                ssem,
+                wr_sem.at[2 * stage + 1],
+                to_band=peer,
+            )
+
+        each(bands - 1, to)
+        plane_r[stage, band] = piece_of(plane_s.at[stage], band)[...]
+
+    def late():
+        to_task(lambda c: msg.at[c, 1], m1.at[zrows], sem_s.at[4], m1_sem.at[z])
+
+    halve(0, sem_s.at[5])
 
     def turn(t):
         off = jnp.where(lax.rem(t, 2) == 1, (t + 1) // 2, 8 - t // 2)
@@ -288,6 +317,8 @@
                     ).astype(BF16)
 
         each(GATES, build)
+        pl.semaphore_wait(plane_ready, rows_x - 1)
+        over_plane(0, sem_s.at[13])
 
         def forward(lv, m_ref, sem):
             def step(t):
@@ -300,7 +331,7 @@
                 rows = pl.ds(pl.multiple_of(k * ROWS, ROWS), ROWS)
                 j = 2 * k + half
                 kinds = idx_r[j, 8 + lv : 9 + lv, :]
-                factors = coefficients(m_ref[rows], kinds, j * ROWS, live[mine, lv])
+                factors = coefficients(m_ref[rows], kinds, j * ROWS, live[lv, mine])
                 for i, f in enumerate(factors):
                     coef[lv, i, rows] = f
                 xts[lv, :, rows] = kinds_ext(kinds)
@@ -308,6 +339,9 @@
             each(8, step)
 
         forward(0, m0, m0_sem)
+        for i in range(1, 4):
+            wait(m0.at[0 : 3 * ROWS], sem_s.at[i])
+        late()
 
         def relay(t):
             k = turn(t)
@@ -351,7 +385,11 @@
             rows = chunk(n)
             q_s[rows] = collect(0, n, d2).astype(BF16)
 
-            @pl.when(band > 0)
+            @pl.when(jnp.logical_and(band > 0, n < NCH // 2))
+            def _():
+                send(q_s.at[rows], q_r.at[rows], sem_s.at[8], q_sem.at[n], gate=me + 2)
+
+            @pl.when(jnp.logical_and(band > 0, n >= NCH // 2))
             def _():
                 send(
                     q_s.at[rows],
@@ -392,8 +430,7 @@
             wacc[:, i * H : (i + 1) * H] += dot_tn(m0[...], gbuf[:, i * H : (i + 1) * H])
         for i in range(4):
             eacc[:, i * H : (i + 1) * H] += dot_nn(xts[0], gbuf[:, i * H : (i + 1) * H])
-        pack_shares(wsend1)
-        scatter_shares(wsend1, wr1, 2 * mine + half, sem_s.at[11], wr_sem.at[1])
+        halve(1, sem_s.at[11])
 
         wait(d4.at[0:OWN], ex_sem.at[2])
 
@@ -416,87 +453,114 @@
                 def _():
                     send(q_s.at[part], out.at[mine], sem_s.at[12], out_sem, gate=2 * k + half)
 
+        over_plane(1, sem_s.at[14])
         each(NCH, second_out)
 
-    wait(wr0.at[0 : GATES - 1], wr_sem.at[0])
+    @pl.when(jnp.logical_not(active))
+    def _():
+        pl.semaphore_wait(plane_ready, rows_x - 1)
+        over_plane(0, sem_s.at[13])
+        for i in range(1, 4):
+            wait(m0.at[0 : 4 * ROWS], sem_s.at[i])
+        late()
+
+        @pl.when(band > 0)
+        def _():
+            def pass_on(n):
+                rows = pl.ds(pl.multiple_of(n * CHUNK, CHUNK), CHUNK)
+                wait(q_r.at[0:CHUNK], q_sem.at[n])
+                send(
+                    q_r.at[rows],
+                    q_r.at[rows],
+                    sem_s.at[8],
+                    q_sem.at[n],
+                    gate=me - 2,
+                    to_band=jnp.maximum(band - 1, 0),
+                )
+
+            each(NCH // 2, pass_on)
+
+    def add_plane(stage):
+        total = plane_r[stage, 0].astype(F32)
+        for i in range(1, bands):
+            total = total + plane_r[stage, i].astype(F32)
+        return total
+
+    wait(plane_r.at[0, 0 : bands - 1], wr_sem.at[1])
 
     @pl.when(active)
     def _():
-        wait(wr1.at[0:7], wr_sem.at[1])
+        wait(plane_r.at[1, 0 : bands - 1], wr_sem.at[3])
+        z_r[z] = (add_plane(0) + add_plane(1)).astype(BF16)
 
     @pl.when(jnp.logical_not(active))
     def _():
-        wait(wr1, wr_sem.at[1])
-
-    total = wr0[0].astype(F32)
-    for i in range(1, GATES):
-        total = total + wr0[i].astype(F32)
-    for i in range(8):
-        total = total + wr1[i].astype(F32)
-    ysend[...] = total.astype(BF16)
-
-    def to_y(i):
-        peer = bx * rows_y + lax.rem(by + 1 + i, rows_y)
-        send(ysend, yr.at[by], sem_s.at[13], wr_sem.at[2], to_band=peer)
-
-    each(rows_y - 1, to_y)
-    yr[by] = ysend[...]
-    wait(yr.at[0 : rows_y - 1], wr_sem.at[2])
-    total = yr[0].astype(F32)
-    for i in range(1, rows_y):
-        total = total + yr[i].astype(F32)
-    if rows_x > 1:
-        xsend[...] = total.astype(BF16)
-
-        def to_x(i):
-            peer = lax.rem(bx + 1 + i, rows_x) * rows_y + by
-            send(xsend, xr.at[bx], sem_s.at[14], wr_sem.at[3], to_band=peer)
-
-        each(rows_x - 1, to_x)
-        xr[bx] = xsend[...]
-        wait(xr.at[0 : rows_x - 1], wr_sem.at[3])
-        total = xr[0].astype(F32)
-        for i in range(1, rows_x):
-            total = total + xr[i].astype(F32)
+        z_r[z] = add_plane(0).astype(BF16)
+
+    def along_z(i):
+        peer = 2 * lax.rem(z + 1 + i, 8) + half
+        send(z_r.at[z], z_r.at[z], sem_s.at[15], wr_sem.at[4], gate=peer)
+
+    each(7, along_z)
+    wait(z_r.at[0:7], wr_sem.at[4])
+    total = z_r[0].astype(F32)
+    for i in range(1, 8):
+        total = total + z_r[i].astype(F32)
     total = total * (1.0 / math.sqrt(CIRC * bands * 2 * ROWS * GATES))
-    ag[me] = total.astype(BF16)
-
-    def to_all(i):
-        peer = lax.rem(me + 1 + i, GATES)
-        send(ag.at[me], ag.at[me], sem_s.at[15], wr_sem.at[4], gate=peer)
-
-    each(GATES - 1, to_all)
-    wait(ag.at[0 : GATES - 1], wr_sem.at[4])
-    for i in range(GATES):
-        wout[16 * i : 16 * i + 16, :] = ag[i, :, : 3 * H].astype(F32)
-        if i < 8:
-            eout[:, ROWS * i : ROWS * (i + 1)] = ag[i, :, 3 * H :].astype(F32)
+    done = piece_of(summed.at[half], band)
+    done[...] = total.astype(BF16)
+
+    def to_plane(i):
+        peer = lax.rem(band + 1 + i, bands)
+        send(done, done, sem_s.at[16], wr_sem.at[5], to_band=peer)
+
+    each(bands - 1, to_plane)
+    wait(plane_r.at[0, 0 : bands - 1], wr_sem.at[5])
+    send(summed.at[half], summed.at[half], sem_s.at[17], wr_sem.at[6], gate=sibling)
+    wait(summed.at[half], wr_sem.at[6])
 
     @pl.when(active)
     def _():
         wait(out.at[0:3], out_sem)
         wait(idx_r.at[0:7], sem_s.at[0])
-        for i in range(1, 5):
-            wait(m0.at[0 : 3 * ROWS], sem_s.at[i])
+        wait(m0.at[0 : 3 * ROWS], sem_s.at[4])
         wait(d1.at[0:OWN], sem_s.at[6])
         wait(d1.at[0:OWN], sem_s.at[7])
         wait(d1.at[0:OWN], sem_s.at[9])
         wait(d1.at[0:OWN], sem_s.at[10])
-        wait(wr0.at[0 : GATES - 1], sem_s.at[11])
+        wait(half_r.at[1], sem_s.at[11])
         wait(q_s.at[0 : 7 * ROWS], sem_s.at[12])
+        wait(plane_r.at[1, 0 : bands - 1], sem_s.at[14])
 
     @pl.when(jnp.logical_not(active))
     def _():
         wait(out, out_sem)
         wait(idx_r.at[0:8], sem_s.at[0])
-        for i in range(1, 5):
-            wait(m0.at[0 : 4 * ROWS], sem_s.at[i])
-
-    wait(wr0.at[0 : GATES - 1], sem_s.at[5])
-    wait(yr.at[0 : rows_y - 1], sem_s.at[13])
-    if rows_x > 1:
-        wait(xr.at[0 : rows_x - 1], sem_s.at[14])
-    wait(ag.at[0 : GATES - 1], sem_s.at[15])
+        wait(m0.at[0 : 4 * ROWS], sem_s.at[4])
+
+        @pl.when(band > 0)
+        def _():
+            wait(q_r.at[0 : OWN // 2], sem_s.at[8])
+
+    wait(half_r.at[0], sem_s.at[5])
+    wait(plane_r.at[0, 0 : bands - 1], sem_s.at[13])
+    wait(z_r.at[0:7], sem_s.at[15])
+    wait(plane_r.at[0, 0 : bands - 1], sem_s.at[16])
+    wait(summed.at[half], sem_s.at[17])
+
+
+def finish_body(moved, summed, out, wout, bout, tout):
+    out[...] = moved[...]
+    for s in range(GATES):
+        for n in range(3):
+            wout[16 * s : 16 * s + 16, n * H : (n + 1) * H] = summed[s % 2, s // 2, n].astype(F32)
+    for s in range(4):
+        ext = summed[s % 2, s // 2, 3].astype(F32)
+        if s != 2:
+            n = min(s, 2)
+            tout[:, n * H : (n + 1) * H] = ext[:8]
+        if s < 3:
+            bout[s * H : (s + 1) * H] = ext[8]
 
 
 def shards(
@@ -512,6 +576,7 @@
 ):
     bands = lax.axis_size("band")
     cols = min(8, bands)
+    piece = (8 // cols, 4 // (bands // cols), 16, H)
     owners = jnp.swapaxes(fanin_owner[:, 0], 2, 3)
     slots = jnp.swapaxes(fanin_slot[:, 0], 2, 3)
     vmem = pl.BlockSpec(memory_space=pltpu.VMEM)
@@ -520,15 +585,14 @@
     def body(*refs):
         kernel_body(bands, cols, *refs)
 
-    out, weight, ext = pl.pallas_call(
+    moved, summed = pl.pallas_call(
         body,
         out_shape=(
             jax.ShapeDtypeStruct((CIRC, ROWS, H), BF16),
-            jax.ShapeDtypeStruct((H, 3 * H), F32),
-            jax.ShapeDtypeStruct((16, 4 * H), F32),
+            jax.ShapeDtypeStruct((2,) + PIECES, BF16),
         ),
         in_specs=[vmem] * 5 + [pl.BlockSpec(memory_space=pltpu.SMEM)] + [vmem] * 3,
-        out_specs=(vmem, vmem, vmem),
+        out_specs=(vmem, vmem),
         scratch_shapes=[
             pltpu.VMEM((CIRC, 16, ROWS), jnp.int32),
             pltpu.VMEM((GATES, 16, ROWS), jnp.int32),
@@ -550,16 +614,12 @@
             pltpu.VMEM((OWN, H), BF16),
             pltpu.VMEM((H, 3 * H), F32),
             pltpu.VMEM((16, 4 * H), F32),
-            pltpu.VMEM((GATES, 16, SHARE), BF16),
-            pltpu.VMEM((GATES, 16, SHARE), BF16),
-            pltpu.VMEM((GATES, 16, SHARE), BF16),
-            pltpu.VMEM((8, 16, SHARE), BF16),
-            pltpu.VMEM((16, SHARE), BF16),
-            pltpu.VMEM((cols, 16, SHARE), BF16),
-            pltpu.VMEM((16, SHARE), BF16),
-            pltpu.VMEM((max(bands // cols, 1), 16, SHARE), BF16),
-            pltpu.VMEM((GATES, 16, SHARE), BF16),
-            dma((16,)),
+            pltpu.VMEM((2, 2) + PIECES, BF16),
+            pltpu.VMEM((2,) + PIECES, BF16),
+            pltpu.VMEM((2,) + PIECES, BF16),
+            pltpu.VMEM((2, bands) + piece, BF16),
+            pltpu.VMEM((8,) + piece, BF16),
+            dma((18,)),
             dma,
             dma((8,)),
             dma,
@@ -569,7 +629,8 @@
             dma((3,)),
             dma((NCH,)),
             dma,
-            dma((5,)),
+            dma((7,)),
+            pltpu.SemaphoreType.REGULAR,
         ],
         compiler_params=pltpu.CompilerParams(
             collective_id=0, has_side_effects=True, vmem_limit_bytes=56 * 1024 * 1024
@@ -581,13 +642,23 @@
         state_grad[:, 0],
         owners,
         slots,
-        live_count[:, 0],
+        live_count[:, 0].T,
         hidden_weight,
-        hidden_bias.reshape(1, 3 * H),
+        hidden_bias,
         type_table,
     )
-    bias = ext[8, : 3 * H]
-    rows = jnp.concatenate([ext[:8, : 2 * H], ext[:8, 3 * H :]], axis=1)
+    out, weight, bias, rows = pl.pallas_call(
+        finish_body,
+        out_shape=(
+            jax.ShapeDtypeStruct((CIRC, ROWS, H), BF16),
+            jax.ShapeDtypeStruct((H, 3 * H), F32),
+            jax.ShapeDtypeStruct((3 * H,), F32),
+            jax.ShapeDtypeStruct((8, 3 * H), F32),
+        ),
+        in_specs=[vmem] * 2,
+        out_specs=(vmem,) * 4,
+        name="results",
+    )(moved, summed)
     return out[:, None], weight, bias, rows
 
 

time: 129 us -> 107 us (0.83)
  Pallas kernels: 118 us -> 106 us
  local copies, waits for them, and re-layouts: 8.41 us -> 0 us
    pallas_call x1, Pallas kernels: 118 us -> 104 us  [shards(): pl.pallas_call(body, out_shape=(jax.ShapeDtypeStruct((CIRC, ROWS, H), BF1...]
    unnamed x6 -> x0, local copies, waits for them, and re-layouts: 4.41 us -> none
    slice x3 -> x0, local copies, waits for them, and re-layouts: 2.76 us -> none  [the longest x2 1.42 us: shards(): rows = jnp.concatenate([ext[:8, :2 * H], ext[:8, 3 * H:]], axis=1)]
    pallas_call x0 -> x1, Pallas kernels: none -> 2.16 us  [shards(): pl.pallas_call(finish_body, out_shape=(jax.ShapeDtypeStruct((CIRC, ROWS,...]
where the time goes in v2:
time: 107 us
  Pallas kernels  106 us (99%)
    pallas_call x1, Pallas kernels, shards(): pl.pallas_call(body, out_shape=(jax.ShapeDtypeStruct((CIRC, ROWS, H), BF1...  104 us
    pallas_call x1, Pallas kernels, shards(): pl.pallas_call(finish_body, out_shape=(jax.ShapeDtypeStruct((CIRC, ROWS,...  2.16 us

profile of v2, /device:TPU:1, one launch (start us, length us, event | category | flops | bytes accessed | tf_op | source)
XLA Modules:
  0.0 106.8 jit_solution(5509773313440517891)
XLA Ops:
  0.6 104.0 %band_passes.1 = (bf16[4,128,256]{2,1,0:T(8,128)(2,1)}, bf16[2,8,4,16,256]{4,3,2,1,0:T(8,128)(2,1)}) custom-call(bf16[4,2,128,256]{3,2,1,0:T(8,128)(2,1)} %bitcast.15, s32[4,2,128]{2,1,0:T(2,128)} %bitcast.19, bf16[4,2,128,256]{3,2,1,0:T(8,128)(2,1)} %bitcast.16, s32[4,2,4,128]{3,2,1,0:T(4,128)} %bitcast.17, s32[4,2,4,128]{3,2,1,0:T(4,128)} %bitcast.18, ...), custom_call_target="tpu_custom_call" | custom-call | tf_op jit(solution)/shard_map/band_passes/pallas_call | solution.py:588
  104.6 2.2 %results.1 = (bf16[4,128,256]{2,1,0:T(8,128)(2,1)}, f32[256,768]{1,0:T(8,128)}, f32[768]{0:T(1024)}, f32[8,768]{1,0:T(8,128)}) custom-call(bf16[4,128,256]{2,1,0:T(8,128)(2,1)} %get-tuple-element.10.moved, bf16[2,8,4,16,256]{4,3,2,1,0:T(8,128)(2,1)} %get-tuple-element.11.summed), custom_call_target="tpu_custom_call" | custom-call | tf_op jit(solution)/shard_map/results/pallas_call | solution.py:650

commit v3 on v2

--- a/solution.py
+++ b/solution.py
@@ -16,6 +16,9 @@
 OWN = 1024
 CHUNK = 256
 NCH = OWN // CHUNK
+PART = 64
+PASSED = 5 * ROWS // 2
+DETOUR = 384
 PIECES = (8, 4, 16, H)
 
 
@@ -73,9 +76,11 @@
     half_r,
     plane_s,
     plane_r,
+    plane_t,
     z_r,
     sem_s,
     idx_sem,
+    fi_sem,
     m0_sem,
     sg0_sem,
     dm_sem,
@@ -83,9 +88,12 @@
     fw_sem,
     ex_sem,
     q_sem,
+    qp_sem,
     out_sem,
     wr_sem,
     plane_ready,
+    pair_ready,
+    below_ready,
 ):
     rows_y = cols
     rows_x = bands // cols
@@ -93,11 +101,20 @@
     band = lax.axis_index("band")
     z = me // 2
     half = lax.rem(me, 2)
-    active = lax.rem(z, 2) == 0
     mine = z // 2
     sibling = me + 1 - 2 * half
     by = lax.rem(band, rows_y)
     bx = band // rows_y
+
+    def parity_of(b):
+        return lax.rem(b + b // rows_y, 2)
+
+    parity = parity_of(band)
+    active = lax.rem(z, 2) == parity
+    below = jnp.maximum(band - 1, 0)
+    below_parity = parity_of(below)
+    beside_y = bx * rows_y + by + 1 - 2 * lax.rem(by, 2)
+    beside_x = (bx + 1 - 2 * lax.rem(bx, 2)) * rows_y + by if rows_x > 1 else beside_y
 
     def send(src, dst, ssem, rsem, gate=None, to_band=None):
         where = {}
@@ -216,37 +233,126 @@
             device_id_type=pl.DeviceIdType.MESH,
         ),
     )
-
-    def to_task(src_of, dst, ssem, rsem):
+    for b in (beside_y, beside_x)[: min(rows_x, 2)]:
+        pl.semaphore_signal(
+            pair_ready, inc=1, device_id={"band": b}, device_id_type=pl.DeviceIdType.MESH
+        )
+
+    @pl.when(band < bands - 1)
+    def _():
+        pl.semaphore_signal(
+            below_ready,
+            inc=1,
+            device_id={"band": jnp.minimum(band + 1, bands - 1)},
+            device_id_type=pl.DeviceIdType.MESH,
+        )
+
+    def block(k):
+        return pl.ds(pl.multiple_of(k * ROWS, ROWS), ROWS)
+
+    def half_block(k, e):
+        return pl.ds(pl.multiple_of(k * ROWS + e * (ROWS // 2), ROWS // 2), ROWS // 2)
+
+    def steps_to(c):
+        return lax.rem(2 * c + parity + 8 - z, 8)
+
+    def gate_of(c):
+        return 2 * (2 * c + parity) + half
+
+    top, bottom = pl.ds(0, ROWS // 2), pl.ds(ROWS // 2, ROWS // 2)
+
+    def to_task(src_of, buf, base, ssem, rsem):
         for c in range(CIRC):
-            local = jnp.logical_and(active, mine == c)
-
-            @pl.when(local)
-            def _():
-                dst[...] = src_of(c)[...]
-
-            @pl.when(jnp.logical_not(local))
-            def _():
-                send(src_of(c), dst, ssem, rsem, gate=4 * c + half)
+            steps = steps_to(c)
+
+            @pl.when(steps == 0)
+            def _():
+                buf[block(base + z)] = src_of(c)[...]
+
+            @pl.when(steps == 4)
+            def _():
+                send(
+                    src_of(c).at[top],
+                    buf.at[half_block(base + z, 0)],
+                    ssem,
+                    rsem.at[z],
+                    gate=gate_of(c),
+                )
+
+            @pl.when(
+                jnp.logical_and(
+                    jnp.logical_and(steps != 0, steps != 4),
+                    jnp.logical_and(steps != 1, steps != 7),
+                )
+            )
+            def _():
+                send(src_of(c), buf.at[block(base + z)], ssem, rsem.at[z], gate=gate_of(c))
+
+    def to_task_by(src_of, buf, base, ssem, rsem):
+        for c in range(CIRC):
+            steps = steps_to(c)
+
+            @pl.when(steps == 1)
+            def _():
+                send(
+                    src_of(c),
+                    buf.at[block(base + z)],
+                    ssem,
+                    rsem.at[z],
+                    gate=gate_of(c),
+                    to_band=beside_y,
+                )
+
+            @pl.when(steps == 4)
+            def _():
+                send(
+                    src_of(c).at[bottom],
+                    buf.at[half_block(base + z, 1)],
+                    ssem,
+                    rsem.at[z],
+                    gate=gate_of(c),
+                    to_band=beside_y,
+                )
+
+            @pl.when(steps == 7)
+            def _():
+                send(
+                    src_of(c),
+                    buf.at[block(base + z)],
+                    ssem,
+                    rsem.at[z],
+                    gate=gate_of(c),
+                    to_band=beside_x,
+                )
+
+    def hand_on(buf, base, ssem, rsem):
+        for steps, b in ((1, beside_y), (7, beside_x), (4, beside_y)):
+            k = lax.rem(z + 8 - steps, 8)
+            place = half_block(base + k, 1) if steps == 4 else block(base + k)
+            wait(buf.at[0 : ROWS // 2] if steps == 4 else buf.at[0:ROWS], rsem.at[k])
+            send(buf.at[place], buf.at[place], ssem, rsem.at[k], to_band=b)
 
     for c in range(CIRC):
-        for h in range(2):
-            local = me == 4 * c + h
-
-            @pl.when(local)
-            def _():
-                idx_r[me] = idx_s[c]
-
-            @pl.when(jnp.logical_not(local))
-            def _():
-                send(idx_s.at[c], idx_r.at[me], sem_s.at[0], idx_sem, gate=4 * c + h)
-
-    zrows = pl.ds(pl.multiple_of(z * ROWS, ROWS), ROWS)
-    to_task(lambda c: msg.at[c, 0], m0.at[zrows], sem_s.at[1], m0_sem.at[z])
-    to_task(lambda c: sg.at[c, 0], sg0.at[zrows], sem_s.at[2], sg0_sem)
-
-    own_rows = pl.ds(pl.multiple_of(half * OWN + z * ROWS, ROWS), ROWS)
-    to_task(lambda c: dm_s.at[c], d1.at[own_rows], sem_s.at[3], dm_sem.at[z])
+
+        @pl.when(steps_to(c) == 0)
+        def _():
+            idx_r[half, z] = idx_s[c]
+
+        @pl.when(steps_to(c) != 0)
+        def _():
+            send(idx_s.at[c], idx_r.at[half, z], sem_s.at[0], idx_sem, gate=gate_of(c))
+
+    first_units = (
+        (lambda c: msg.at[c, 0], m0, 0, sem_s.at[1], m0_sem),
+        (lambda c: sg.at[c, 0], sg0, 0, sem_s.at[2], sg0_sem),
+        (lambda c: dm_s.at[c], d1, 8 * half, sem_s.at[3], dm_sem),
+    )
+    last_unit = (lambda c: msg.at[c, 1], m1, 0, sem_s.at[4], m1_sem)
+    for unit in first_units:
+        to_task(*unit)
+    pl.semaphore_wait(pair_ready, min(rows_x, 2))
+    for unit in first_units:
+        to_task_by(*unit)
     py, px = 8 // rows_y, 4 // rows_x
 
     def piece_of(ref, to):
@@ -266,7 +372,7 @@
             half_s.at[stage, 1 - half], half_r.at[stage], ssem, wr_sem.at[2 * stage], gate=sibling
         )
 
-    def over_plane(stage, ssem):
+    def over_plane(stage, dst, ssem):
         wait(half_r.at[stage], wr_sem.at[2 * stage])
         for p in range(8):
             plane_s[stage, p] = (
@@ -277,17 +383,18 @@
             peer = lax.rem(band + 1 + i, bands)
             send(
                 piece_of(plane_s.at[stage], peer),
-                plane_r.at[stage, band],
+                dst,
                 ssem,
                 wr_sem.at[2 * stage + 1],
                 to_band=peer,
             )
 
         each(bands - 1, to)
-        plane_r[stage, band] = piece_of(plane_s.at[stage], band)[...]
+        dst[...] = piece_of(plane_s.at[stage], band)[...]
 
     def late():
-        to_task(lambda c: msg.at[c, 1], m1.at[zrows], sem_s.at[4], m1_sem.at[z])
+        to_task(*last_unit)
+        to_task_by(*last_unit)
 
     halve(0, sem_s.at[5])
 
@@ -297,11 +404,12 @@
 
     @pl.when(active)
     def _():
-        wait(idx_r.at[0 : GATES - 1], idx_sem)
+        wait(idx_r.at[0, 0:7], idx_sem)
+        send(idx_r.at[half], idx_r.at[half], sem_s.at[18], fi_sem, gate=sibling)
 
         def build(j):
-            tile = idx_r[j]
-            col = pl.ds(pl.multiple_of(lax.rem(j, 2) * OWN + (j // 2) * ROWS, ROWS), ROWS)
+            tile = idx_r[j // 8, lax.rem(j, 8)]
+            col = pl.ds(pl.multiple_of(j * ROWS, ROWS), ROWS)
             spot = iota((ROWS, ROWS), 0)
             block = 2 * iota((8, ROWS), 0) + half
             for lv in (1, 0):
@@ -316,9 +424,11 @@
                         spot == at[k : k + 1, :], 1.0, 0.0
                     ).astype(BF16)
 
-        each(GATES, build)
+        each(8, lambda k: build(8 * half + k))
+        wait(idx_r.at[0], fi_sem)
+        each(8, lambda k: build(8 - 8 * half + k))
         pl.semaphore_wait(plane_ready, rows_x - 1)
-        over_plane(0, sem_s.at[13])
+        over_plane(0, plane_r.at[band], sem_s.at[13])
 
         def forward(lv, m_ref, sem):
             def step(t):
@@ -330,7 +440,7 @@
 
                 rows = pl.ds(pl.multiple_of(k * ROWS, ROWS), ROWS)
                 j = 2 * k + half
-                kinds = idx_r[j, 8 + lv : 9 + lv, :]
+                kinds = idx_r[half, k, 8 + lv : 9 + lv, :]
                 factors = coefficients(m_ref[rows], kinds, j * ROWS, live[lv, mine])
                 for i, f in enumerate(factors):
                     coef[lv, i, rows] = f
@@ -354,7 +464,7 @@
             send(d1.at[rows], d1.at[rows], sem_s.at[6], fw_sem, gate=sibling)
 
         each(8, relay)
-        wait(sg0.at[0 : 7 * ROWS], sg0_sem)
+        each(7, lambda i: wait(sg0.at[0:ROWS], sg0_sem.at[lax.rem(z + 1 + i, 8)]))
         wait(d1.at[0:OWN], fw_sem)
 
         def chunk(n):
@@ -373,6 +483,10 @@
         def collect(lv, n, src):
             return dot_nn(sel[lv, chunk(n)], src[...])
 
+        @pl.when(band > 0)
+        def _():
+            pl.semaphore_wait(below_ready, 1)
+
         def first_zero(n):
             s = sg0[chunk(n)].astype(F32) + collect(1, n, d1)
             s0[chunk(n)] = s
@@ -385,19 +499,34 @@
             rows = chunk(n)
             q_s[rows] = collect(0, n, d2).astype(BF16)
 
-            @pl.when(jnp.logical_and(band > 0, n < NCH // 2))
-            def _():
-                send(q_s.at[rows], q_r.at[rows], sem_s.at[8], q_sem.at[n], gate=me + 2)
-
-            @pl.when(jnp.logical_and(band > 0, n >= NCH // 2))
-            def _():
-                send(
-                    q_s.at[rows],
-                    q_r.at[rows],
-                    sem_s.at[8],
-                    q_sem.at[n],
-                    to_band=jnp.maximum(band - 1, 0),
-                )
+            @pl.when(band > 0)
+            def _():
+                def part(e):
+                    i = n * (CHUNK // PART) + e
+                    place = pl.ds(pl.multiple_of(i * PART, PART), PART)
+
+                    @pl.when(i < DETOUR // PART)
+                    def _():
+                        send(
+                            q_s.at[place],
+                            q_r.at[place],
+                            sem_s.at[8],
+                            qp_sem.at[i],
+                            gate=2 * (2 * mine + 1 - parity) + half,
+                        )
+
+                    @pl.when(i >= DETOUR // PART)
+                    def _():
+                        send(
+                            q_s.at[place],
+                            q_r.at[place],
+                            sem_s.at[8],
+                            q_sem.at[n],
+                            gate=2 * (2 * mine + below_parity) + half,
+                            to_band=below,
+                        )
+
+                each(CHUNK // PART, part)
 
             @pl.when(band == bands - 1)
             def _():
@@ -453,49 +582,54 @@
                 def _():
                     send(q_s.at[part], out.at[mine], sem_s.at[12], out_sem, gate=2 * k + half)
 
-        over_plane(1, sem_s.at[14])
-        each(NCH, second_out)
+        each(NCH // 2, second_out)
+        over_plane(1, plane_t.at[band // 2], sem_s.at[14])
+        each(NCH // 2, lambda n: second_out(NCH // 2 + n))
 
     @pl.when(jnp.logical_not(active))
     def _():
+        for _, buf, base, ssem, rsem in first_units:
+            hand_on(buf, base, ssem, rsem)
         pl.semaphore_wait(plane_ready, rows_x - 1)
-        over_plane(0, sem_s.at[13])
+        over_plane(0, plane_r.at[band], sem_s.at[13])
         for i in range(1, 4):
-            wait(m0.at[0 : 4 * ROWS], sem_s.at[i])
+            wait(m0.at[0 : 4 * ROWS + PASSED], sem_s.at[i])
         late()
+        hand_on(*last_unit[1:])
 
         @pl.when(band > 0)
         def _():
-            def pass_on(n):
-                rows = pl.ds(pl.multiple_of(n * CHUNK, CHUNK), CHUNK)
-                wait(q_r.at[0:CHUNK], q_sem.at[n])
+            def pass_on(i):
+                place = pl.ds(pl.multiple_of(i * PART, PART), PART)
+                wait(q_r.at[0:PART], qp_sem.at[i])
                 send(
-                    q_r.at[rows],
-                    q_r.at[rows],
+                    q_r.at[place],
+                    q_r.at[place],
                     sem_s.at[8],
-                    q_sem.at[n],
-                    gate=me - 2,
-                    to_band=jnp.maximum(band - 1, 0),
+                    q_sem.at[i // (CHUNK // PART)],
+                    gate=2 * (2 * mine + below_parity) + half,
+                    to_band=below,
                 )
 
-            each(NCH // 2, pass_on)
-
-    def add_plane(stage):
-        total = plane_r[stage, 0].astype(F32)
-        for i in range(1, bands):
-            total = total + plane_r[stage, i].astype(F32)
-        return total
-
-    wait(plane_r.at[0, 0 : bands - 1], wr_sem.at[1])
+            pl.semaphore_wait(below_ready, 1)
+            each(DETOUR // PART, pass_on)
+
+    wait(plane_r.at[0 : bands - 1], wr_sem.at[1])
 
     @pl.when(active)
     def _():
-        wait(plane_r.at[1, 0 : bands - 1], wr_sem.at[3])
-        z_r[z] = (add_plane(0) + add_plane(1)).astype(BF16)
+        wait(plane_t.at[0 : bands // 2 - 1], wr_sem.at[3])
 
     @pl.when(jnp.logical_not(active))
     def _():
-        z_r[z] = add_plane(0).astype(BF16)
+        wait(plane_t.at[0 : bands // 2], wr_sem.at[3])
+
+    total = plane_r[0].astype(F32)
+    for i in range(1, bands):
+        total = total + plane_r[i].astype(F32)
+    for i in range(bands // 2):
+        total = total + plane_t[i].astype(F32)
+    z_r[z] = total.astype(BF16)
 
     def along_z(i):
         peer = 2 * lax.rem(z + 1 + i, 8) + half
@@ -515,14 +649,15 @@
         send(done, done, sem_s.at[16], wr_sem.at[5], to_band=peer)
 
     each(bands - 1, to_plane)
-    wait(plane_r.at[0, 0 : bands - 1], wr_sem.at[5])
+    wait(plane_r.at[0 : bands - 1], wr_sem.at[5])
     send(summed.at[half], summed.at[half], sem_s.at[17], wr_sem.at[6], gate=sibling)
     wait(summed.at[half], wr_sem.at[6])
 
     @pl.when(active)
     def _():
         wait(out.at[0:3], out_sem)
-        wait(idx_r.at[0:7], sem_s.at[0])
+        wait(idx_r.at[0, 0:3], sem_s.at[0])
+        wait(idx_r.at[0], sem_s.at[18])
         wait(m0.at[0 : 3 * ROWS], sem_s.at[4])
         wait(d1.at[0:OWN], sem_s.at[6])
         wait(d1.at[0:OWN], sem_s.at[7])
@@ -530,22 +665,22 @@
         wait(d1.at[0:OWN], sem_s.at[10])
         wait(half_r.at[1], sem_s.at[11])
         wait(q_s.at[0 : 7 * ROWS], sem_s.at[12])
-        wait(plane_r.at[1, 0 : bands - 1], sem_s.at[14])
+        wait(plane_r.at[0 : bands - 1], sem_s.at[14])
 
     @pl.when(jnp.logical_not(active))
     def _():
         wait(out, out_sem)
-        wait(idx_r.at[0:8], sem_s.at[0])
-        wait(m0.at[0 : 4 * ROWS], sem_s.at[4])
+        wait(idx_r.at[0, 0:4], sem_s.at[0])
+        wait(m0.at[0 : 4 * ROWS + PASSED], sem_s.at[4])
 
         @pl.when(band > 0)
         def _():
-            wait(q_r.at[0 : OWN // 2], sem_s.at[8])
+            wait(q_r.at[0:DETOUR], sem_s.at[8])
 
     wait(half_r.at[0], sem_s.at[5])
-    wait(plane_r.at[0, 0 : bands - 1], sem_s.at[13])
+    wait(plane_r.at[0 : bands - 1], sem_s.at[13])
     wait(z_r.at[0:7], sem_s.at[15])
-    wait(plane_r.at[0, 0 : bands - 1], sem_s.at[16])
+    wait(plane_r.at[0 : bands - 1], sem_s.at[16])
     wait(summed.at[half], sem_s.at[17])
 
 
@@ -595,7 +730,7 @@
         out_specs=(vmem, vmem),
         scratch_shapes=[
             pltpu.VMEM((CIRC, 16, ROWS), jnp.int32),
-            pltpu.VMEM((GATES, 16, ROWS), jnp.int32),
+            pltpu.VMEM((2, 8, 16, ROWS), jnp.int32),
             pltpu.VMEM((32, 3 * H), BF16),
             pltpu.VMEM((OWN, H), BF16),
             pltpu.VMEM((OWN, H), BF16),
@@ -617,19 +752,24 @@
             pltpu.VMEM((2, 2) + PIECES, BF16),
             pltpu.VMEM((2,) + PIECES, BF16),
             pltpu.VMEM((2,) + PIECES, BF16),
-            pltpu.VMEM((2, bands) + piece, BF16),
+            pltpu.VMEM((bands,) + piece, BF16),
+            pltpu.VMEM((max(bands // 2, 1),) + piece, BF16),
             pltpu.VMEM((8,) + piece, BF16),
-            dma((18,)),
+            dma((19,)),
+            dma,
             dma,
             dma((8,)),
-            dma,
+            dma((8,)),
             dma((8,)),
             dma((8,)),
             dma,
             dma((3,)),
             dma((NCH,)),
+            dma((DETOUR // PART,)),
             dma,
             dma((7,)),
+            pltpu.SemaphoreType.REGULAR,
+            pltpu.SemaphoreType.REGULAR,
             pltpu.SemaphoreType.REGULAR,
         ],
         compiler_params=pltpu.CompilerParams(

time: 107 us -> 99.3 us (0.928)
  Pallas kernels: 106 us -> 98.5 us
    pallas_call x1, Pallas kernels: 104 us -> 96.3 us  [shards(): pl.pallas_call(body, out_shape=(jax.ShapeDtypeStruct((CIRC, ROWS, H), BF1...]
where the time goes in v3:
time: 99.3 us; the launch traced here: 99.1 us
  Pallas kernels  98.5 us (99%)
    pallas_call x1, Pallas kernels, shards(): pl.pallas_call(body, out_shape=(jax.ShapeDtypeStruct((CIRC, ROWS, H), BF1...  96.3 us
    pallas_call x1, Pallas kernels, shards(): pl.pallas_call(finish_body, out_shape=(jax.ShapeDtypeStruct((CIRC, ROWS,...  2.16 us

profile of v3, /device:TPU:1, one launch (start us, length us, event | category | flops | bytes accessed | tf_op | source)
XLA Modules:
  0.0 99.1 jit_solution(4700842431284169460)
XLA Ops:
  0.6 96.3 %band_passes.1 = (bf16[4,128,256]{2,1,0:T(8,128)(2,1)}, bf16[2,8,4,16,256]{4,3,2,1,0:T(8,128)(2,1)}) custom-call(bf16[4,2,128,256]{3,2,1,0:T(8,128)(2,1)} %bitcast.15, s32[4,2,128]{2,1,0:T(2,128)} %bitcast.19, bf16[4,2,128,256]{3,2,1,0:T(8,128)(2,1)} %bitcast.16, s32[4,2,4,128]{3,2,1,0:T(4,128)} %bitcast.17, s32[4,2,4,128]{3,2,1,0:T(4,128)} %bitcast.18, ...), custom_call_target="tpu_custom_call" | custom-call | tf_op jit(solution)/shard_map/band_passes/pallas_call | solution.py:723
  97.0 2.2 %results.1 = (bf16[4,128,256]{2,1,0:T(8,128)(2,1)}, f32[256,768]{1,0:T(8,128)}, f32[768]{0:T(1024)}, f32[8,768]{1,0:T(8,128)}) custom-call(bf16[4,128,256]{2,1,0:T(8,128)(2,1)} %get-tuple-element.10.moved, bf16[2,8,4,16,256]{4,3,2,1,0:T(8,128)(2,1)} %get-tuple-element.11.summed), custom_call_target="tpu_custom_call" | custom-call | tf_op jit(solution)/shard_map/results/pallas_call | solution.py:790

commit v4 on v3

--- a/solution.py
+++ b/solution.py
@@ -19,7 +19,7 @@
 PART = 64
 PASSED = 5 * ROWS // 2
 DETOUR = 384
-PIECES = (8, 4, 16, H)
+PIECES = (4, 8, 16, H)
 
 
 def iota(shape, dim):
@@ -72,11 +72,12 @@
     q_r,
     wacc,
     eacc,
+    msg1,
+    sg1,
     half_s,
     half_r,
     plane_s,
     plane_r,
-    plane_t,
     z_r,
     sem_s,
     idx_sem,
@@ -91,9 +92,11 @@
     qp_sem,
     out_sem,
     wr_sem,
-    plane_ready,
+    ax_sem,
+    own_sem,
     pair_ready,
     below_ready,
+    plane_ready,
 ):
     rows_y = cols
     rows_x = bands // cols
@@ -141,6 +144,11 @@
 
         lax.fori_loop(0, count, step, 0)
 
+    load_m = pltpu.make_async_copy(msg.at[:, 1], msg1, own_sem.at[0])
+    load_s = pltpu.make_async_copy(sg.at[:, 1], sg1, own_sem.at[1])
+    load_m.start()
+    load_s.start()
+
     barrier = pltpu.get_barrier_semaphore()
 
     def greet(**where):
@@ -148,7 +156,8 @@
             barrier, inc=1, device_id=where, device_id_type=pl.DeviceIdType.MESH
         )
 
-    each(GATES - 1, lambda i: greet(gate=lax.rem(me + 1 + i, GATES)))
+    each(7, lambda i: greet(gate=lax.rem(me + 2 + 2 * i, GATES)))
+    greet(gate=sibling)
     each(rows_y - 1, lambda i: greet(band=bx * rows_y + lax.rem(by + 1 + i, rows_y)))
     if rows_x > 1:
         each(rows_x - 1, lambda i: greet(band=lax.rem(bx + 1 + i, rows_x) * rows_y + by))
@@ -210,10 +219,10 @@
     eacc[...] = jnp.zeros_like(eacc)
 
     def level_one(c):
-        m = msg[c, 1]
+        m = msg1[c]
         kinds = types[c, 1:2, :]
         factors = coefficients(m, kinds, me * ROWS, live[1, c])
-        dr, dz, dc, dn, down = grads(sg[c, 1].astype(F32), factors)
+        dr, dz, dc, dn, down = grads(sg1[c].astype(F32), factors)
         dm_s[c] = down
         ext = kinds_ext(kinds)
         for i, g in enumerate((dr, dz, dc)):
@@ -221,9 +230,11 @@
         for i, g in enumerate((dr, dz, dc, dn)):
             eacc[:, i * H : (i + 1) * H] += dot_nn(ext, g)
 
+    load_m.wait()
+    load_s.wait()
     each(CIRC, level_one)
 
-    pl.semaphore_wait(barrier, GATES - 1 + rows_y - 1 + rows_x - 1 + 2)
+    pl.semaphore_wait(barrier, 8 + rows_y - 1 + rows_x - 1 + 2)
     each(
         rows_x - 1,
         lambda i: pl.semaphore_signal(
@@ -267,7 +278,7 @@
 
             @pl.when(steps == 0)
             def _():
-                buf[block(base + z)] = src_of(c)[...]
+                pltpu.make_async_copy(src_of(c), buf.at[block(base + z)], rsem.at[z]).start()
 
             @pl.when(steps == 4)
             def _():
@@ -343,60 +354,66 @@
             send(idx_s.at[c], idx_r.at[half, z], sem_s.at[0], idx_sem, gate=gate_of(c))
 
     first_units = (
+        (lambda c: dm_s.at[c], d1, 8 * half, sem_s.at[3], dm_sem),
         (lambda c: msg.at[c, 0], m0, 0, sem_s.at[1], m0_sem),
         (lambda c: sg.at[c, 0], sg0, 0, sem_s.at[2], sg0_sem),
-        (lambda c: dm_s.at[c], d1, 8 * half, sem_s.at[3], dm_sem),
     )
-    last_unit = (lambda c: msg.at[c, 1], m1, 0, sem_s.at[4], m1_sem)
-    for unit in first_units:
+    last_unit = (lambda c: msg1.at[c], m1, 0, sem_s.at[4], m1_sem)
+    to_task(*first_units[0])
+    pl.semaphore_wait(pair_ready, min(rows_x, 2))
+    to_task_by(*first_units[0])
+    for unit in first_units[1:]:
+        to_task_by(*unit)
         to_task(*unit)
-    pl.semaphore_wait(pair_ready, min(rows_x, 2))
-    for unit in first_units:
-        to_task_by(*unit)
     py, px = 8 // rows_y, 4 // rows_x
 
+    def x_part(ref, x):
+        return ref.at[pl.ds(x * px, px)]
+
     def piece_of(ref, to):
-        return ref.at[pl.ds(lax.rem(to, rows_y) * py, py), pl.ds((to // rows_y) * px, px)]
-
-    def halve(stage, ssem):
+        return ref.at[pl.ds((to // rows_y) * px, px), pl.ds(lax.rem(to, rows_y) * py, py)]
+
+    def halve():
         for i in range(GATES):
             for n in range(3):
-                half_s[stage, i % 2, i // 2, n] = wacc[
-                    16 * i : 16 * i + 16, n * H : (n + 1) * H
-                ].astype(BF16)
+                half_s[i % 2, n, i // 2] = wacc[16 * i : 16 * i + 16, n * H : (n + 1) * H].astype(
+                    BF16
+                )
             if i < 4:
-                half_s[stage, i % 2, i // 2, 3] = eacc[:, i * H : (i + 1) * H].astype(BF16)
+                half_s[i % 2, 3, i // 2] = eacc[:, i * H : (i + 1) * H].astype(BF16)
             else:
-                half_s[stage, i % 2, i // 2, 3] = jnp.zeros((16, H), BF16)
-        send(
-            half_s.at[stage, 1 - half], half_r.at[stage], ssem, wr_sem.at[2 * stage], gate=sibling
-        )
-
-    def over_plane(stage, dst, ssem):
-        wait(half_r.at[stage], wr_sem.at[2 * stage])
-        for p in range(8):
-            plane_s[stage, p] = (
-                half_s[stage, half, p].astype(F32) + half_r[stage, p].astype(F32)
-            ).astype(BF16)
+                half_s[i % 2, 3, i // 2] = jnp.zeros((16, H), BF16)
+        send(half_s.at[1 - half], half_r, sem_s.at[5], wr_sem.at[0], gate=sibling)
+
+    def over_plane():
+        wait(half_r, wr_sem.at[0])
+        for n in range(4):
+            plane_s[n] = (half_s[half, n].astype(F32) + half_r[n].astype(F32)).astype(BF16)
+        pl.semaphore_wait(plane_ready, rows_x - 1)
 
         def to(i):
             peer = lax.rem(band + 1 + i, bands)
-            send(
-                piece_of(plane_s.at[stage], peer),
-                dst,
-                ssem,
-                wr_sem.at[2 * stage + 1],
-                to_band=peer,
-            )
+            send(piece_of(plane_s, peer), plane_r.at[band], sem_s.at[11], wr_sem.at[1], to_band=peer)
 
         each(bands - 1, to)
-        dst[...] = piece_of(plane_s.at[stage], band)[...]
+        plane_r[band] = piece_of(plane_s, band)[...]
+
+    def along_ring():
+        wait(plane_r.at[0 : bands - 1], wr_sem.at[1])
+        total = plane_r[0].astype(F32)
+        for i in range(1, bands):
+            total = total + plane_r[i].astype(F32)
+        z_r[z] = total.astype(BF16)
+
+        def to(i):
+            peer = 2 * lax.rem(z + 1 + i, 8) + half
+            send(z_r.at[z], z_r.at[z], sem_s.at[15], wr_sem.at[4], gate=peer)
+
+        each(7, to)
 
     def late():
         to_task(*last_unit)
         to_task_by(*last_unit)
-
-    halve(0, sem_s.at[5])
 
     def turn(t):
         off = jnp.where(lax.rem(t, 2) == 1, (t + 1) // 2, 8 - t // 2)
@@ -427,17 +444,12 @@
         each(8, lambda k: build(8 * half + k))
         wait(idx_r.at[0], fi_sem)
         each(8, lambda k: build(8 - 8 * half + k))
-        pl.semaphore_wait(plane_ready, rows_x - 1)
-        over_plane(0, plane_r.at[band], sem_s.at[13])
 
         def forward(lv, m_ref, sem):
             def step(t):
                 k = turn(t)
 
-                @pl.when(t > 0)
-                def _():
-                    wait(m_ref.at[0:ROWS], sem.at[k])
-
+                wait(m_ref.at[0:ROWS], sem.at[k])
                 rows = pl.ds(pl.multiple_of(k * ROWS, ROWS), ROWS)
                 j = 2 * k + half
                 kinds = idx_r[half, k, 8 + lv : 9 + lv, :]
@@ -457,14 +469,11 @@
             k = turn(t)
             rows = pl.ds(pl.multiple_of(half * OWN + k * ROWS, ROWS), ROWS)
 
-            @pl.when(t > 0)
-            def _():
-                wait(d1.at[0:ROWS], dm_sem.at[k])
-
+            wait(d1.at[0:ROWS], dm_sem.at[k])
             send(d1.at[rows], d1.at[rows], sem_s.at[6], fw_sem, gate=sibling)
 
         each(8, relay)
-        each(7, lambda i: wait(sg0.at[0:ROWS], sg0_sem.at[lax.rem(z + 1 + i, 8)]))
+        each(8, lambda i: wait(sg0.at[0:ROWS], sg0_sem.at[i]))
         wait(d1.at[0:OWN], fw_sem)
 
         def chunk(n):
@@ -545,9 +554,9 @@
         each(NCH, second_one)
 
         for i in range(3):
-            wacc[:, i * H : (i + 1) * H] = dot_tn(m1[...], gbuf[:, i * H : (i + 1) * H])
+            wacc[:, i * H : (i + 1) * H] += dot_tn(m1[...], gbuf[:, i * H : (i + 1) * H])
         for i in range(4):
-            eacc[:, i * H : (i + 1) * H] = dot_nn(xts[1], gbuf[:, i * H : (i + 1) * H])
+            eacc[:, i * H : (i + 1) * H] += dot_nn(xts[1], gbuf[:, i * H : (i + 1) * H])
         wait(d3.at[0:OWN], ex_sem.at[1])
 
         def second_zero(n):
@@ -559,7 +568,7 @@
             wacc[:, i * H : (i + 1) * H] += dot_tn(m0[...], gbuf[:, i * H : (i + 1) * H])
         for i in range(4):
             eacc[:, i * H : (i + 1) * H] += dot_nn(xts[0], gbuf[:, i * H : (i + 1) * H])
-        halve(1, sem_s.at[11])
+        halve()
 
         wait(d4.at[0:OWN], ex_sem.at[2])
 
@@ -568,30 +577,32 @@
             wait(q_s, sem_s.at[8])
 
         def second_out(n):
-            rows = chunk(n)
-            q_s[rows] = collect(0, n, d4).astype(BF16)
-            for e in range(2):
-                k = 2 * n + e
-                part = pl.ds(pl.multiple_of(k * ROWS, ROWS), ROWS)
-
-                @pl.when(k == z)
-                def _():
-                    out[mine] = q_s[part]
-
-                @pl.when(k != z)
-                def _():
-                    send(q_s.at[part], out.at[mine], sem_s.at[12], out_sem, gate=2 * k + half)
-
-        each(NCH // 2, second_out)
-        over_plane(1, plane_t.at[band // 2], sem_s.at[14])
+            q_s[chunk(n)] = collect(0, n, d4).astype(BF16)
+
+        def deliver(k):
+            @pl.when(k == z)
+            def _():
+                out[mine] = q_s[block(k)]
+
+            @pl.when(k != z)
+            def _():
+                send(q_s.at[block(k)], out.at[mine], sem_s.at[12], out_sem, gate=2 * k + half)
+
+        def second_out_now(n):
+            second_out(n)
+            deliver(2 * n)
+            deliver(2 * n + 1)
+
+        each(NCH // 2, second_out_now)
+        over_plane()
         each(NCH // 2, lambda n: second_out(NCH // 2 + n))
+        along_ring()
+        each(4, lambda k: deliver(4 + k))
 
     @pl.when(jnp.logical_not(active))
     def _():
         for _, buf, base, ssem, rsem in first_units:
             hand_on(buf, base, ssem, rsem)
-        pl.semaphore_wait(plane_ready, rows_x - 1)
-        over_plane(0, plane_r.at[band], sem_s.at[13])
         for i in range(1, 4):
             wait(m0.at[0 : 4 * ROWS + PASSED], sem_s.at[i])
         late()
@@ -614,28 +625,10 @@
             pl.semaphore_wait(below_ready, 1)
             each(DETOUR // PART, pass_on)
 
-    wait(plane_r.at[0 : bands - 1], wr_sem.at[1])
-
-    @pl.when(active)
-    def _():
-        wait(plane_t.at[0 : bands // 2 - 1], wr_sem.at[3])
-
-    @pl.when(jnp.logical_not(active))
-    def _():
-        wait(plane_t.at[0 : bands // 2], wr_sem.at[3])
-
-    total = plane_r[0].astype(F32)
-    for i in range(1, bands):
-        total = total + plane_r[i].astype(F32)
-    for i in range(bands // 2):
-        total = total + plane_t[i].astype(F32)
-    z_r[z] = total.astype(BF16)
-
-    def along_z(i):
-        peer = 2 * lax.rem(z + 1 + i, 8) + half
-        send(z_r.at[z], z_r.at[z], sem_s.at[15], wr_sem.at[4], gate=peer)
-
-    each(7, along_z)
+        halve()
+        over_plane()
+        along_ring()
+
     wait(z_r.at[0:7], wr_sem.at[4])
     total = z_r[0].astype(F32)
     for i in range(1, 8):
@@ -646,11 +639,25 @@
 
     def to_plane(i):
         peer = lax.rem(band + 1 + i, bands)
-        send(done, done, sem_s.at[16], wr_sem.at[5], to_band=peer)
+        send(done, done, sem_s.at[16], ax_sem.at[bx], to_band=peer)
 
     each(bands - 1, to_plane)
-    wait(plane_r.at[0 : bands - 1], wr_sem.at[5])
-    send(summed.at[half], summed.at[half], sem_s.at[17], wr_sem.at[6], gate=sibling)
+
+    def to_sibling(i):
+        x = lax.rem(bx + i, rows_x)
+        there = x_part(summed.at[half], x)
+
+        @pl.when(i == 0)
+        def _():
+            wait(plane_r.at[0 : rows_y - 1], ax_sem.at[x])
+
+        @pl.when(i > 0)
+        def _():
+            wait(plane_r.at[0:rows_y], ax_sem.at[x])
+
+        send(there, there, sem_s.at[17], wr_sem.at[6], gate=sibling)
+
+    each(rows_x, to_sibling)
     wait(summed.at[half], wr_sem.at[6])
 
     @pl.when(active)
@@ -663,9 +670,7 @@
         wait(d1.at[0:OWN], sem_s.at[7])
         wait(d1.at[0:OWN], sem_s.at[9])
         wait(d1.at[0:OWN], sem_s.at[10])
-        wait(half_r.at[1], sem_s.at[11])
         wait(q_s.at[0 : 7 * ROWS], sem_s.at[12])
-        wait(plane_r.at[0 : bands - 1], sem_s.at[14])
 
     @pl.when(jnp.logical_not(active))
     def _():
@@ -677,8 +682,8 @@
         def _():
             wait(q_r.at[0:DETOUR], sem_s.at[8])
 
-    wait(half_r.at[0], sem_s.at[5])
-    wait(plane_r.at[0 : bands - 1], sem_s.at[13])
+    wait(half_r, sem_s.at[5])
+    wait(plane_r.at[0 : bands - 1], sem_s.at[11])
     wait(z_r.at[0:7], sem_s.at[15])
     wait(plane_r.at[0 : bands - 1], sem_s.at[16])
     wait(summed.at[half], sem_s.at[17])
@@ -688,9 +693,9 @@
     out[...] = moved[...]
     for s in range(GATES):
         for n in range(3):
-            wout[16 * s : 16 * s + 16, n * H : (n + 1) * H] = summed[s % 2, s // 2, n].astype(F32)
+            wout[16 * s : 16 * s + 16, n * H : (n + 1) * H] = summed[s % 2, n, s // 2].astype(F32)
     for s in range(4):
-        ext = summed[s % 2, s // 2, 3].astype(F32)
+        ext = summed[s % 2, 3, s // 2].astype(F32)
         if s != 2:
             n = min(s, 2)
             tout[:, n * H : (n + 1) * H] = ext[:8]
@@ -711,10 +716,12 @@
 ):
     bands = lax.axis_size("band")
     cols = min(8, bands)
-    piece = (8 // cols, 4 // (bands // cols), 16, H)
+    rows_x = bands // cols
+    py, px = 8 // cols, 4 // rows_x
     owners = jnp.swapaxes(fanin_owner[:, 0], 2, 3)
     slots = jnp.swapaxes(fanin_slot[:, 0], 2, 3)
     vmem = pl.BlockSpec(memory_space=pltpu.VMEM)
+    hbm = pl.BlockSpec(memory_space=pl.ANY)
     dma = pltpu.SemaphoreType.DMA
 
     def body(*refs):
@@ -726,7 +733,7 @@
             jax.ShapeDtypeStruct((CIRC, ROWS, H), BF16),
             jax.ShapeDtypeStruct((2,) + PIECES, BF16),
         ),
-        in_specs=[vmem] * 5 + [pl.BlockSpec(memory_space=pltpu.SMEM)] + [vmem] * 3,
+        in_specs=[hbm, vmem, hbm, vmem, vmem, pl.BlockSpec(memory_space=pltpu.SMEM)] + [vmem] * 3,
         out_specs=(vmem, vmem),
         scratch_shapes=[
             pltpu.VMEM((CIRC, 16, ROWS), jnp.int32),
@@ -749,12 +756,13 @@
             pltpu.VMEM((OWN, H), BF16),
             pltpu.VMEM((H, 3 * H), F32),
             pltpu.VMEM((16, 4 * H), F32),
-            pltpu.VMEM((2, 2) + PIECES, BF16),
+            pltpu.VMEM((CIRC, ROWS, H), BF16),
+            pltpu.VMEM((CIRC, ROWS, H), BF16),
             pltpu.VMEM((2,) + PIECES, BF16),
-            pltpu.VMEM((2,) + PIECES, BF16),
-            pltpu.VMEM((bands,) + piece, BF16),
-            pltpu.VMEM((max(bands // 2, 1),) + piece, BF16),
-            pltpu.VMEM((8,) + piece, BF16),
+            pltpu.VMEM(PIECES, BF16),
+            pltpu.VMEM(PIECES, BF16),
+            pltpu.VMEM((bands, px, py, 16, H), BF16),
+            pltpu.VMEM((8, px, py, 16, H), BF16),
             dma((19,)),
             dma,
             dma,
@@ -768,6 +776,8 @@
             dma((DETOUR // PART,)),
             dma,
             dma((7,)),
+            dma((rows_x,)),
+            dma((2,)),
             pltpu.SemaphoreType.REGULAR,
             pltpu.SemaphoreType.REGULAR,
             pltpu.SemaphoreType.REGULAR,

time: 99.3 us -> 97 us (0.977)
  Pallas kernels: 98.5 us -> 96.2 us
    pallas_call x1, Pallas kernels: 96.3 us -> 94 us  [shards(): pl.pallas_call(body, out_shape=(jax.ShapeDtypeStruct((CIRC, ROWS, H), BF1...]
where the time goes in v4:
time: 97 us; the launch traced here: 96.8 us
  Pallas kernels  96.2 us (99%)
    pallas_call x1, Pallas kernels, shards(): pl.pallas_call(body, out_shape=(jax.ShapeDtypeStruct((CIRC, ROWS, H), BF1...  94 us
    pallas_call x1, Pallas kernels, shards(): pl.pallas_call(finish_body, out_shape=(jax.ShapeDtypeStruct((CIRC, ROWS,...  2.16 us

profile of v4, /device:TPU:1, one launch (start us, length us, event | category | flops | bytes accessed | tf_op | source)
XLA Modules:
  0.0 96.8 jit_solution(16825804280347510208)
XLA Ops:
  0.6 94.0 %band_passes.1 = (bf16[4,128,256]{2,1,0:T(8,128)(2,1)}, bf16[2,4,8,16,256]{4,3,2,1,0:T(8,128)(2,1)}) custom-call(bf16[4,2,128,256]{3,2,1,0:T(8,128)(2,1)} %bitcast.15, s32[4,2,128]{2,1,0:T(2,128)} %bitcast.19, bf16[4,2,128,256]{3,2,1,0:T(8,128)(2,1)} %bitcast.16, s32[4,2,4,128]{3,2,1,0:T(4,128)} %bitcast.17, s32[4,2,4,128]{3,2,1,0:T(4,128)} %bitcast.18, ...), custom_call_target="tpu_custom_call" | custom-call | tf_op jit(solution)/shard_map/band_passes/pallas_call | solution.py:730
  94.7 2.2 %results.1 = (bf16[4,128,256]{2,1,0:T(8,128)(2,1)}, f32[256,768]{1,0:T(8,128)}, f32[768]{0:T(1024)}, f32[8,768]{1,0:T(8,128)}) custom-call(bf16[4,128,256]{2,1,0:T(8,128)(2,1)} %get-tuple-element.10.moved, bf16[2,4,8,16,256]{4,3,2,1,0:T(8,128)(2,1)} %get-tuple-element.11.summed), custom_call_target="tpu_custom_call" | custom-call | tf_op jit(solution)/shard_map/results/pallas_call | solution.py:800

commit v5 on v4

--- a/solution.py
+++ b/solution.py
@@ -373,6 +373,34 @@
     def piece_of(ref, to):
         return ref.at[pl.ds((to // rows_y) * px, px), pl.ds(lax.rem(to, rows_y) * py, py)]
 
+    if rows_y == 8:
+        flat = half == 0
+        place = jnp.where(flat, band, bx * rows_y + z)
+        height = jnp.where(flat, z, by)
+    else:
+        flat = half >= 0
+        place, height = band, z
+
+    def send_in_plane(src, dst, ssem, rsem, to):
+        send(
+            src,
+            dst,
+            ssem,
+            rsem,
+            gate=jnp.where(flat, me, 2 * lax.rem(to, rows_y) + half),
+            to_band=jnp.where(flat, to, (to // rows_y) * rows_y + by),
+        )
+
+    def send_across(src, dst, ssem, rsem, to):
+        send(
+            src,
+            dst,
+            ssem,
+            rsem,
+            gate=jnp.where(flat, 2 * to + half, me),
+            to_band=jnp.where(flat, band, bx * rows_y + lax.rem(to, rows_y)),
+        )
+
     def halve():
         for i in range(GATES):
             for n in range(3):
@@ -392,22 +420,24 @@
         pl.semaphore_wait(plane_ready, rows_x - 1)
 
         def to(i):
-            peer = lax.rem(band + 1 + i, bands)
-            send(piece_of(plane_s, peer), plane_r.at[band], sem_s.at[11], wr_sem.at[1], to_band=peer)
+            peer = lax.rem(place + 1 + i, bands)
+            send_in_plane(
+                piece_of(plane_s, peer), plane_r.at[place], sem_s.at[11], wr_sem.at[1], peer
+            )
 
         each(bands - 1, to)
-        plane_r[band] = piece_of(plane_s, band)[...]
+        plane_r[place] = piece_of(plane_s, place)[...]
 
     def along_ring():
         wait(plane_r.at[0 : bands - 1], wr_sem.at[1])
         total = plane_r[0].astype(F32)
         for i in range(1, bands):
             total = total + plane_r[i].astype(F32)
-        z_r[z] = total.astype(BF16)
+        z_r[height] = total.astype(BF16)
 
         def to(i):
-            peer = 2 * lax.rem(z + 1 + i, 8) + half
-            send(z_r.at[z], z_r.at[z], sem_s.at[15], wr_sem.at[4], gate=peer)
+            peer = lax.rem(height + 1 + i, 8)
+            send_across(z_r.at[height], z_r.at[height], sem_s.at[15], wr_sem.at[4], peer)
 
         each(7, to)
 
@@ -588,16 +618,11 @@
             def _():
                 send(q_s.at[block(k)], out.at[mine], sem_s.at[12], out_sem, gate=2 * k + half)
 
-        def second_out_now(n):
-            second_out(n)
-            deliver(2 * n)
-            deliver(2 * n + 1)
-
-        each(NCH // 2, second_out_now)
         over_plane()
+        each(NCH // 2, second_out)
         each(NCH // 2, lambda n: second_out(NCH // 2 + n))
         along_ring()
-        each(4, lambda k: deliver(4 + k))
+        each(8, deliver)
 
     @pl.when(jnp.logical_not(active))
     def _():
@@ -634,12 +659,12 @@
     for i in range(1, 8):
         total = total + z_r[i].astype(F32)
     total = total * (1.0 / math.sqrt(CIRC * bands * 2 * ROWS * GATES))
-    done = piece_of(summed.at[half], band)
+    done = piece_of(summed.at[half], place)
     done[...] = total.astype(BF16)
 
     def to_plane(i):
-        peer = lax.rem(band + 1 + i, bands)
-        send(done, done, sem_s.at[16], ax_sem.at[bx], to_band=peer)
+        peer = lax.rem(place + 1 + i, bands)
+        send_in_plane(done, done, sem_s.at[16], ax_sem.at[bx], peer)
 
     each(bands - 1, to_plane)
 

time: 97 us -> 96.1 us (level)
  Pallas kernels: 96.2 us -> 95.2 us
where the time goes in v5:
time: 96.1 us; the launch traced here: 95.9 us
  Pallas kernels  95.2 us (99%)
    pallas_call x1, Pallas kernels, shards(): pl.pallas_call(body, out_shape=(jax.ShapeDtypeStruct((CIRC, ROWS, H), BF1...  93.1 us
    pallas_call x1, Pallas kernels, shards(): pl.pallas_call(finish_body, out_shape=(jax.ShapeDtypeStruct((CIRC, ROWS,...  2.16 us

profile of v5, /device:TPU:1, one launch (start us, length us, event | category | flops | bytes accessed | tf_op | source)
XLA Modules:
  0.0 95.9 jit_solution(10194752362635989523)
XLA Ops:
  0.6 93.1 %band_passes.1 = (bf16[4,128,256]{2,1,0:T(8,128)(2,1)}, bf16[2,4,8,16,256]{4,3,2,1,0:T(8,128)(2,1)}) custom-call(bf16[4,2,128,256]{3,2,1,0:T(8,128)(2,1)} %bitcast.15, s32[4,2,128]{2,1,0:T(2,128)} %bitcast.19, bf16[4,2,128,256]{3,2,1,0:T(8,128)(2,1)} %bitcast.16, s32[4,2,4,128]{3,2,1,0:T(4,128)} %bitcast.17, s32[4,2,4,128]{3,2,1,0:T(4,128)} %bitcast.18, ...), custom_call_target="tpu_custom_call" | custom-call | tf_op jit(solution)/shard_map/band_passes/pallas_call | solution.py:755
  93.7 2.2 %results.1 = (bf16[4,128,256]{2,1,0:T(8,128)(2,1)}, f32[256,768]{1,0:T(8,128)}, f32[768]{0:T(1024)}, f32[8,768]{1,0:T(8,128)}) custom-call(bf16[4,128,256]{2,1,0:T(8,128)(2,1)} %get-tuple-element.10.moved, bf16[2,4,8,16,256]{4,3,2,1,0:T(8,128)(2,1)} %get-tuple-element.11.summed), custom_call_target="tpu_custom_call" | custom-call | tf_op jit(solution)/shard_map/results/pallas_call | solution.py:825

commit v6 on v5

--- a/solution.py
+++ b/solution.py
@@ -18,7 +18,7 @@
 NCH = OWN // CHUNK
 PART = 64
 PASSED = 5 * ROWS // 2
-DETOUR = 384
+DETOUR = 320
 PIECES = (4, 8, 16, H)
 
 
@@ -491,8 +491,6 @@
             each(8, step)
 
         forward(0, m0, m0_sem)
-        for i in range(1, 4):
-            wait(m0.at[0 : 3 * ROWS], sem_s.at[i])
         late()
 
         def relay(t):
@@ -690,7 +688,8 @@
         wait(out.at[0:3], out_sem)
         wait(idx_r.at[0, 0:3], sem_s.at[0])
         wait(idx_r.at[0], sem_s.at[18])
-        wait(m0.at[0 : 3 * ROWS], sem_s.at[4])
+        for i in range(1, 5):
+            wait(m0.at[0 : 3 * ROWS], sem_s.at[i])
         wait(d1.at[0:OWN], sem_s.at[6])
         wait(d1.at[0:OWN], sem_s.at[7])
         wait(d1.at[0:OWN], sem_s.at[9])

time: 96.1 us -> 95.7 us (level)
  no operation moved by 1% of the time
where the time goes in v6:
time: 95.7 us; the launch traced here: 95.5 us
  Pallas kernels  94.9 us (99%)
    pallas_call x1, Pallas kernels, shards(): pl.pallas_call(body, out_shape=(jax.ShapeDtypeStruct((CIRC, ROWS, H), BF1...  92.7 us
    pallas_call x1, Pallas kernels, shards(): pl.pallas_call(finish_body, out_shape=(jax.ShapeDtypeStruct((CIRC, ROWS,...  2.16 us

profile of v6, /device:TPU:1, one launch (start us, length us, event | category | flops | bytes accessed | tf_op | source)
XLA Modules:
  0.0 95.5 jit_solution(12852524408359086133)
XLA Ops:
  0.6 92.7 %band_passes.1 = (bf16[4,128,256]{2,1,0:T(8,128)(2,1)}, bf16[2,4,8,16,256]{4,3,2,1,0:T(8,128)(2,1)}) custom-call(bf16[4,2,128,256]{3,2,1,0:T(8,128)(2,1)} %bitcast.15, s32[4,2,128]{2,1,0:T(2,128)} %bitcast.19, bf16[4,2,128,256]{3,2,1,0:T(8,128)(2,1)} %bitcast.16, s32[4,2,4,128]{3,2,1,0:T(4,128)} %bitcast.17, s32[4,2,4,128]{3,2,1,0:T(4,128)} %bitcast.18, ...), custom_call_target="tpu_custom_call" | custom-call | tf_op jit(solution)/shard_map/band_passes/pallas_call | solution.py:754
  93.4 2.2 %results.1 = (bf16[4,128,256]{2,1,0:T(8,128)(2,1)}, f32[256,768]{1,0:T(8,128)}, f32[768]{0:T(1024)}, f32[8,768]{1,0:T(8,128)}) custom-call(bf16[4,128,256]{2,1,0:T(8,128)(2,1)} %get-tuple-element.10.moved, bf16[2,4,8,16,256]{4,3,2,1,0:T(8,128)(2,1)} %get-tuple-element.11.summed), custom_call_target="tpu_custom_call" | custom-call | tf_op jit(solution)/shard_map/results/pallas_call | solution.py:824
